TPU v7x, 256 devices: a whole 4x4x8 slice. The times are simulated.
256 devices in a mesh: ta: 16 (over z_lo, y, core), ha: 16 (over z_hi, x).
Axes of the slice: x: 4, y: 4, z: 8 (z_hi: 4, z_lo: 2; z = z_hi * 2 + z_lo), core: 2. Of those that a mesh axis runs over, the one named last changes fastest.
Arguments:
- queries: bfloat16 [64, 64, 16, 1536], P('ta', 'ha'), may hold values from -5 to 5
- keys_values: bfloat16 [2, 64, 64, 16, 1536], P(None, 'ta', 'ha'), may hold values from -5 to 5
- upstream: bfloat16 [64, 64, 16, 1536], P('ta', 'ha'), may hold values from -6 to 6
- out_weight: bfloat16 [1536, 1536], P('ha'), may hold values from -0.15625 to 0.15625
- windows: int32 [12, 3], replicated, may hold values from 1 to 3, as said below
- bucket_owner: int32 [48], replicated, may hold values from 0 to 15, as said below
Outputs:
- d_queries: bfloat16 [64, 64, 16, 1536], P('ta', 'ha')
- d_keys_values: bfloat16 [2, 64, 64, 16, 1536], P(None, 'ta', 'ha')
- d_weight_owned: float32 [96, 32, 1536], P('ha', 'ta')
Inputs may be any that keep to these rules, and one draw needn't show every extreme that they name: `windows`: sizes are odd; some head, drawn from the seed, has 3 along all three dimensions, and some other head has 1 along at least one dimension. `bucket_owner`: each owner holds at most 6 buckets and some owner holds exactly 6.
All inputs are finite; a program needn't handle non-finite values.
Results may differ from a plain program's by a relative error of at most 0.007.
Values may be sent and summed in bfloat16 or wider, within the bound.
A program may use at most 128 MiB of HBM per device.

v0:
```python
import jax
import jax.numpy as jnp
from jax import lax
from jax.experimental import pallas as pl
from jax.experimental.pallas import tpu as pltpu
from jax.sharding import PartitionSpec as P

HEADS = 12
HEAD_DIM = 128
ACROSS = (((1,), (1,)), ((), ()))


def place():
    ta, ha = lax.axis_index("ta"), lax.axis_index("ha")
    return ta // 8, ta // 2 % 4, ta % 2, ha // 4, ha % 4


def at_place(z_lo, y, core, z_hi, x):
    return {"ta": z_lo * 8 + y * 2 + core, "ha": z_hi * 4 + x}


class Copies:
    def __init__(self, send, recv):
        self.send, self.recv, self.made = send, recv, []

    def start(self, src, dst, device):
        index = len(self.made)
        made = pltpu.make_async_remote_copy(
            src_ref=src,
            dst_ref=dst,
            send_sem=self.send.at[index],
            recv_sem=self.recv.at[index],
            device_id=device,
            device_id_type=pl.DeviceIdType.MESH,
        )
        made.start()
        self.made.append(made)
        return made

    def drain(self):
        for made in self.made:
            made.wait_send()


class RingSum:
    def __init__(self, copies, src, pos, after, before, bufs):
        self.copies, self.src, self.pos, self.after, self.before = copies, src, pos, after, before
        self.left, self.right, self.via_left, self.via_right, self.stage = bufs

    def start(self):
        pos, src, start = self.pos, self.src, self.copies.start
        far = (pos + 2) % 4
        self.first = [
            start(src.at[far, 0], self.via_left, self.after),
            start(src.at[far, 1], self.via_right, self.before),
        ]
        self.left_1 = start(src.at[(pos + 1) % 4, 1], self.left.at[1], self.after)
        self.right_0 = start(src.at[(pos + 3) % 4, 0], self.right.at[0], self.before)

    def middle(self):
        pos, src = self.pos, self.src
        made = []
        for index, (via, goal, dst, device) in enumerate(
            (
                (self.via_left, (pos + 1) % 4, self.left, self.after),
                (self.via_right, (pos + 3) % 4, self.right, self.before),
            )
        ):
            self.first[index].wait_recv()
            total = via[...].astype(jnp.float32) + src[goal, index].astype(jnp.float32)
            self.stage[index] = total.astype(self.stage.dtype)
            made.append(self.copies.start(self.stage.at[index], dst.at[index], device))
        self.left_0, self.right_1 = made

    def end(self, half):
        for made in ((self.right_0, self.left_0), (self.left_1, self.right_1))[half]:
            made.wait_recv()
        return (
            self.src[self.pos, half].astype(jnp.float32)
            + self.left[half].astype(jnp.float32)
            + self.right[half].astype(jnp.float32)
        )


def ring_buffers(rows, columns):
    return [
        pltpu.VMEM((2, rows, columns), jnp.bfloat16),
        pltpu.VMEM((2, rows, columns), jnp.bfloat16),
        pltpu.VMEM((rows, columns), jnp.bfloat16),
        pltpu.VMEM((rows, columns), jnp.bfloat16),
        pltpu.VMEM((2, rows, columns), jnp.bfloat16),
    ]


class RingGather:
    def __init__(self, copies, block, pos, after, before):
        self.copies, self.block, self.pos, self.after, self.before = copies, block, pos, after, before

    def start(self):
        own = self.block(self.pos, 0, 4)
        self.from_before = self.copies.start(own, own, self.after)
        self.from_after = self.copies.start(own, own, self.before)

    def middle(self):
        self.from_before.wait_recv()
        part = self.block((self.pos + 3) % 4, 0, 2)
        self.far_before = self.copies.start(part, part, self.after)
        self.from_after.wait_recv()
        part = self.block((self.pos + 1) % 4, 2, 2)
        self.far_after = self.copies.start(part, part, self.before)

    def end(self):
        self.far_before.wait_recv()
        self.far_after.wait_recv()


def window_bits(need):
    time_index, height_index = lax.axis_index("ta"), lax.axis_index("ha")
    key = lax.broadcasted_iota(jnp.int32, (96, 256), 0)
    token = lax.broadcasted_iota(jnp.int32, (96, 256), 1)
    row_gap = jnp.abs((token >> 4 & 3) - (key >> 4) + 1)
    tile_gap = jnp.abs((token >> 3 & 1) - (key >> 3 & 1))
    row = height_index * 4 + (key >> 4) - 1
    base = jnp.where((row_gap > 1) | (row < 0) | (row >= 64), 8, row_gap * 2 + tile_gap * 4)
    for f in range(6):
        time_gap = jnp.abs((token >> 6) - f + 1)
        frame = time_index * 4 + f - 1
        outside = (time_gap > 1) | (frame < 0) | (frame >= 64)
        need[f * 96 : f * 96 + 96] = base | jnp.where(outside, 8, time_gap)


def block_kernel(q, kv_in, up, weight_in, windows, dq, dkv_out, fin, *refs):
    f32, bf16 = jnp.float32, jnp.bfloat16
    kv, dkv, weight, probs_all, need, at, at_in, up_in = refs[:8]
    from_left, from_right, from_above, from_below = refs[8:12]
    first_a, first_b, second_a, second_b, pair_sums, pair_in, tall, tall_in = refs[12:20]
    rings = [refs[20 + 5 * i : 25 + 5 * i] for i in range(4)]
    send, recv, local_sem = refs[40:]
    z_lo, y, core, z_hi, x = place()
    ta, ha = lax.axis_index("ta"), lax.axis_index("ha")
    partner = at_place(z_lo, y, 1 - core, z_hi, x)
    y_after, y_before = (at_place(z_lo, (y + s) % 4, core, z_hi, x) for s in (1, 3))
    x_peers = [at_place(z_lo, y, core, z_hi, (x + s) % 4) for s in (1, 2, 3)]
    x_after, _, x_before = x_peers
    low_peer = at_place(1 - z_lo, y, core, z_hi, x)
    high_peers = [at_place(z_lo, y, core, (z_hi + s) % 4, x) for s in (1, 2, 3)]
    next_row, last_row = ({"ta": ta, "ha": (ha + s) % 16} for s in (1, 15))
    next_frame, last_frame = ({"ta": (ta + s) % 16, "ha": ha} for s in (1, 15))

    own_copy = pltpu.make_async_copy(kv_in, kv.at[:, pl.ds(1, 4), pl.ds(1, 4)], local_sem)
    own_copy.start()
    peers = [partner, y_after, y_before, *x_peers, low_peer, *high_peers]
    peers += [next_row, last_row, next_frame, last_frame]
    barrier = pltpu.get_barrier_semaphore()
    for peer in peers:
        pl.semaphore_signal(barrier, inc=1, device_id=peer, device_id_type=pl.DeviceIdType.MESH)
    window_bits(need)
    pl.semaphore_wait(barrier, len(peers))

    copies = Copies(send, recv)
    start = copies.start
    mine = pl.ds(1, 4)
    rows_in = [
        start(kv_in.at[:, :, 3], kv.at[:, mine, 0], next_row),
        start(kv_in.at[:, :, 0], kv.at[:, mine, 5], last_row),
    ]
    frames_in = [
        start(kv_in.at[:, 3], kv.at[:, 0, mine], next_frame),
        start(kv_in.at[:, 0], kv.at[:, 5, mine], last_frame),
    ]
    quarter = pl.ds(pl.multiple_of(y * 384, 384), 384)
    piece = weight_in.at[pl.ds(pl.multiple_of(core * 48, 16), 48), quarter]
    weight[z_hi, x, core, :, quarter] = weight_in[pl.ds(pl.multiple_of(core * 48, 16), 48), quarter]
    pieces_in = [start(piece, weight.at[z_hi, x, core, :, quarter], peer) for peer in high_peers]
    up_swap = start(up, up_in, partner)

    def over_x(p, begin, size):
        return weight.at[pl.ds(begin, size), p, core, :, quarter]

    def over_y(p, begin, size):
        return weight.at[pl.ds(begin, size), :, core, :, pl.ds(pl.multiple_of(p * 384, 384), 384)]

    gather_x = RingGather(copies, over_x, x, x_after, x_before)
    gather_y = RingGather(copies, over_y, y, y_after, y_before)
    for made in pieces_in:
        made.wait_recv()
    gather_x.start()
    for made in rows_in:
        made.wait_recv()
    corners_in = []
    for frame, goal, device in ((4, 0, next_frame), (1, 5, last_frame)):
        for row in (0, 5):
            corners_in.append(start(kv.at[:, frame, row], kv.at[:, goal, row], device))
    gather_x.middle()
    gather_x.end()
    gather_y.start()
    swaps = [start(over_y(y, 0, 4), over_y(y, 0, 4), partner)]
    own_copy.wait()
    for made in (*frames_in, *corners_in):
        made.wait_recv()

    out_row = lax.broadcasted_iota(jnp.int32, (128, 128), 0)
    feature = lax.broadcasted_iota(jnp.int32, (128, 128), 1)
    group = out_row >> 3
    turn = (group >> 2 & 1) * 8 + (group & 3) * 2 + (group >> 3)
    wanted = (out_row >> 1 & 3) * 32 + turn * 2 + (out_row & 1)
    order = (wanted == feature).astype(bf16)
    eye = (out_row == feature).astype(bf16)
    scaling = HEAD_DIM ** (-0.5)

    def forward(pair, carry):
        outs = []
        for side in range(2):
            head = pair * 2 + side
            cols = pl.ds(pl.multiple_of(head * 128, 128), 128)
            keys, values = (kv[i, :, :, :, cols].reshape(576, 128) for i in range(2))
            block = 15 - sum(((windows[head, a] - 1) // 2) << a for a in range(3))
            scores = lax.dot_general(keys, q[:, cols], ACROSS, preferred_element_type=f32)
            scores = jnp.where((need[...] & block) == 0, scores, -1e30)
            highest = jnp.max(scores, axis=0, keepdims=True)
            weights = jnp.exp2((scores - highest) * (scaling * 1.4426950408889634))
            probs = weights * (1.0 / jnp.sum(weights, axis=0, keepdims=True))
            probs_all[head] = probs
            values_t = lax.dot_general(order, values, ACROSS, preferred_element_type=f32).astype(bf16)
            out = jnp.dot(values_t, probs.astype(bf16), preferred_element_type=f32)
            outs.append(out.reshape(16, 8, 256))
        at[:, pl.ds(pl.multiple_of(pair * 16, 16), 16), :] = jnp.concatenate(outs, axis=1).astype(bf16)
        return carry

    def backward(pair, carry):
        begin = pl.multiple_of(pair * 256, 16)
        rows = weight_rows[pl.ds(begin, 256), :]
        grad_pair = lax.dot_general(up[...], rows, ACROSS, preferred_element_type=f32).astype(bf16)
        for side in range(2):
            head = pair * 2 + side
            cols = pl.ds(pl.multiple_of(head * 128, 128), 128)
            keys, values = (kv[i, :, :, :, cols].reshape(576, 128) for i in range(2))
            grad = grad_pair[:, side * 128 : side * 128 + 128]
            probs = probs_all[head]
            grad_probs = lax.dot_general(values, grad, ACROSS, preferred_element_type=f32)
            delta = jnp.sum(probs * grad_probs, axis=0, keepdims=True)
            grad_scores = (probs * (grad_probs - delta) * scaling).astype(bf16)
            keys_t = lax.dot_general(eye, keys, ACROSS, preferred_element_type=f32).astype(bf16)
            dq[:, cols] = jnp.dot(keys_t, grad_scores, preferred_element_type=f32).T.astype(bf16)
            grad_keys = jnp.dot(grad_scores, q[:, cols], preferred_element_type=f32).astype(bf16)
            grad_values = jnp.dot(probs.astype(bf16), grad, preferred_element_type=f32).astype(bf16)
            dkv[0, :, :, :, cols] = grad_keys.reshape(6, 6, 16, 128)
            dkv[1, :, :, :, cols] = grad_values.reshape(6, 6, 16, 128)
        return carry

    lax.fori_loop(0, 6, forward, 0)
    at_swap = start(at.at[pl.ds((1 - core) * 8, 8)], at_in, partner)
    gather_y.middle()
    for step in (3, 1):
        part = over_y((y + step) % 4, 0, 4)
        swaps.append(start(part, part, partner))
    up_swap.wait_recv()
    at_swap.wait_recv()

    def product(part, begin, width):
        a = at[pl.ds(core * 8 + part * 4, 4)].reshape(384, 256)
        b = at_in[part * 4 : part * 4 + 4].reshape(384, 256)
        total = jnp.dot(a, up[:, begin : begin + width], preferred_element_type=f32)
        total += jnp.dot(b, up_in[:, begin : begin + width], preferred_element_type=f32)
        return total.astype(bf16)

    ring_a = RingSum(copies, first_a, y, y_after, y_before, rings[0])
    ring_b = RingSum(copies, first_b, x, x_after, x_before, rings[1])
    ring_c = RingSum(copies, second_a, x, x_after, x_before, rings[2])
    ring_d = RingSum(copies, second_b, y, y_after, y_before, rings[3])
    for goal in range(4):
        block = product(1, goal * 384, 384)
        for half in range(2):
            first_b[goal, half] = block[half * 192 : half * 192 + 192]
    ring_b.start()
    for half in range(2):
        block = product(0, half * 768, 768)
        for goal in range(4):
            first_a[goal, half] = block[goal * 96 : goal * 96 + 96]
    ring_a.start()
    gather_y.end()
    part = over_y((y + 2) % 4, 0, 4)
    swaps.append(start(part, part, partner))
    for made in swaps:
        made.wait_recv()
    weight_rows = weight.reshape(1536, 1536)
    lax.fori_loop(0, 3, backward, 0)
    ring_b.middle()
    ring_a.middle()
    lax.fori_loop(3, 6, backward, 0)
    sides = [
        start(dkv.at[:, 5], from_left, next_frame),
        start(dkv.at[:, 0], from_right, last_frame),
    ]
    inner = pl.ds(1, 2)
    outer = [
        start(dkv.at[:, pl.ds(2, 2), 5], from_above.at[:, inner], next_row),
        start(dkv.at[:, pl.ds(2, 2), 0], from_below.at[:, inner], last_row),
    ]
    for half in range(2):
        block = ring_b.end(half).astype(bf16)
        for goal in range(2):
            for row in range(2):
                begin = goal * 96 + row * 48
                second_b[half * 2 + goal, row] = block[begin : begin + 48]
    ring_d.start()
    for half in range(2):
        block = ring_a.end(half).astype(bf16)
        for goal in range(2):
            for row in range(2):
                second_a[half * 2 + goal, row] = block[row * 48 : row * 48 + 48, goal * 384 : goal * 384 + 384]
    ring_c.start()
    for made, frame, came, first in ((sides[0], 1, from_left, 0), (sides[1], 4, from_right, 3)):
        made.wait_recv()
        for i in range(2):
            total = dkv[i, frame].astype(f32) + came[i].astype(f32)
            came[i] = total.astype(bf16)
        outer.append(start(came.at[:, 5], from_above.at[:, first], next_row))
        outer.append(start(came.at[:, 0], from_below.at[:, first], last_row))
    ring_d.middle()
    ring_c.middle()
    for part, ring in ((1, ring_d), (0, ring_c)):
        for row in range(2):
            pair_sums[part, row * 48 : row * 48 + 48] = ring.end(row).astype(bf16)
    low = start(pair_sums.at[1 - z_lo], pair_in, low_peer)
    low.wait_recv()
    total = pair_sums[z_lo].astype(f32) + pair_in[...].astype(f32)
    tall[...] = total.astype(bf16)
    highs = [start(tall, tall_in.at[i], high_peers[i]) for i in range(3)]
    for i in range(2):
        dkv_out[i, :, 1:3] = dkv[i, 1:5, 2:4]
        for f in (1, 2):
            for r in (0, 3):
                dkv_out[i, f, r] = dkv[i, f + 1, r + 1]
        for f, came in ((0, from_left), (3, from_right)):
            dkv_out[i, f] = came[i, 1:5]
    for made in outer:
        made.wait_recv()
    for i in range(2):
        for f in range(4):
            for r, came in ((0, from_above), (3, from_below)):
                dkv_out[i, f, r] = (dkv_out[i, f, r].astype(f32) + came[i, f].astype(f32)).astype(bf16)
    for i in range(3):
        highs[i].wait_recv()
        total += tall_in[i].astype(f32)
    fin[x] = (total * 0.00390625).astype(bf16)
    lasts = [start(fin.at[x], fin.at[x], peer) for peer in x_peers]
    for made in lasts:
        made.wait_recv()
    copies.drain()


def run_block(q, kv, up, weight, windows):
    bf16 = jnp.bfloat16
    vmem = pl.BlockSpec(memory_space=pltpu.VMEM)
    return pl.pallas_call(
        block_kernel,
        out_shape=[
            jax.ShapeDtypeStruct((256, 1536), bf16),
            jax.ShapeDtypeStruct((2, 4, 4, 16, 1536), bf16),
            jax.ShapeDtypeStruct((4, 96, 384), bf16),
        ],
        in_specs=[vmem, pl.BlockSpec(memory_space=pl.ANY), vmem, vmem, pl.BlockSpec(memory_space=pltpu.SMEM)],
        out_specs=[vmem, vmem, vmem],
        scratch_shapes=[
            pltpu.VMEM((2, 6, 6, 16, 1536), bf16),
            pltpu.VMEM((2, 6, 6, 16, 1536), bf16),
            pltpu.VMEM((4, 4, 2, 48, 1536), bf16),
            pltpu.VMEM((12, 576, 256), jnp.float32),
            pltpu.VMEM((576, 256), jnp.int32),
            pltpu.VMEM((16, 96, 256), bf16),
            pltpu.VMEM((8, 96, 256), bf16),
            pltpu.VMEM((256, 1536), bf16),
            pltpu.VMEM((2, 6, 16, 1536), bf16),
            pltpu.VMEM((2, 6, 16, 1536), bf16),
            pltpu.VMEM((2, 4, 16, 1536), bf16),
            pltpu.VMEM((2, 4, 16, 1536), bf16),
            pltpu.VMEM((4, 2, 96, 768), bf16),
            pltpu.VMEM((4, 2, 192, 384), bf16),
            pltpu.VMEM((4, 2, 48, 384), bf16),
            pltpu.VMEM((4, 2, 48, 384), bf16),
            pltpu.VMEM((2, 96, 384), bf16),
            pltpu.VMEM((96, 384), bf16),
            pltpu.VMEM((96, 384), bf16),
            pltpu.VMEM((3, 96, 384), bf16),
            *ring_buffers(96, 768),
            *ring_buffers(192, 384),
            *ring_buffers(48, 384),
            *ring_buffers(48, 384),
            pltpu.SemaphoreType.DMA((64,)),
            pltpu.SemaphoreType.DMA((64,)),
            pltpu.SemaphoreType.DMA,
        ],
        compiler_params=pltpu.CompilerParams(
            collective_id=1, has_side_effects=True, vmem_limit_bytes=56 * 1024 * 1024
        ),
    )(q, kv, up, weight, windows)


def owned_slots(fin, bucket_owner, height_index):
    bucket_ids = jnp.arange(48, dtype=jnp.int32)
    same_owner = bucket_owner[None, :] == bucket_owner[:, None]
    ranking = jnp.sum((same_owner & (bucket_ids[None, :] < bucket_ids[:, None])).astype(jnp.int32), axis=1)
    slot = jnp.where(bucket_owner == height_index, ranking, -1)
    chosen = jnp.repeat(slot * 2, 2) + jnp.tile(jnp.arange(2, dtype=jnp.int32), 48)
    pick = (chosen[None, :] == jnp.arange(12, dtype=jnp.int32)[:, None]).astype(jnp.bfloat16)
    owned = jnp.einsum("sr,xrc->sxc", pick, fin, preferred_element_type=jnp.float32)
    return owned.reshape(6, 2, 1536)


def per_device(queries, keys_values, upstream, out_weight, windows, bucket_owner):
    grad_query, grad_pairs, fin = run_block(
        queries.reshape(256, 1536), keys_values, upstream.reshape(256, 1536), out_weight, windows
    )
    owned = owned_slots(fin, bucket_owner, lax.axis_index("ha"))
    return grad_query.reshape(queries.shape), grad_pairs, owned


def solution(mesh):
    return jax.shard_map(
        per_device,
        mesh=mesh,
        in_specs=(
            P("ta", "ha", None, None),
            P(None, "ta", "ha", None, None),
            P("ta", "ha", None, None),
            P("ha", None),
            P(),
            P(),
        ),
        out_specs=(P("ta", "ha", None, None), P(None, "ta", "ha", None, None), P("ha", "ta", None)),
        check_vma=False,
    )
```

profile of v0, /device:TPU:6, one launch (start us, length us, event | category | flops | bytes accessed | tf_op | source)
XLA Modules:
  0.0 133.9 jit_solution(1102163682837948364)
XLA Ops:
  0.6 0.9 convert_reduce_fusion
  1.5 0.7 fusion.5
  2.2 1.4 %copy.12.windows = s32[12,3]{1,0:T(8,128)} copy(s32[12,3]{0,1:T(4,128)} %param.10) | data formatting | bytes 288 | tf_op args[4]
  3.6 0.1 iota_add_fusion
  3.6 0.1 add.11
  3.8 125.0 %shard_map.85 = (bf16[256,1536]{1,0:T(8,128)(2,1)}, bf16[2,4,4,16,1536]{4,3,2,1,0:T(8,128)(2,1)}, bf16[4,96,384]{2,1,0:T(8,128)(2,1)}) custom-call(bf16[256,1536]{1,0:T(8,128)(2,1)} %bitcast.8, bf16[2,4,4,16,1536]{4,3,2,1,0:T(8,128)(2,1)} %kv_in.1, bf16[256,1536]{1,0:T(8,128)(2,1)} %bitcast.9, bf16[96,1536]{1,0:T(8,128)(2,1)} %weight_in.1, s32[12,3]{1,0:T(8,128)} %copy.12.windows), custom_call_target="tpu_custom_call" | custom-call | tf_op jit(solution)/shard_map/pallas_call | solution.py:356
  128.8 0.0 copy-start
  128.8 1.2 fusion.2
  130.1 0.7 reshape.34
  130.7 2.1 %copy.16 = bf16[4,4,16,1536]{3,2,1,0:T(8,128)(2,1)} copy(bf16[4,4,16,1536]{3,2,1,0:T(8,128)(2,1)} %bitcast.7) | data formatting | bytes 1572864
  132.8 0.0 copy-done
  132.8 1.1 copy.17
  (1 shorter events, 0.0 us)
Async XLA Ops:
  128.8 4.0 %copy-start = (bf16[2,4,4,16,1536]{4,3,2,1,0:T(8,128)(2,1)S(1)}, bf16[2,4,4,16,1536]{4,3,2,1,0:T(8,128)(2,1)}, u32[]{:S(2)}) copy-start(bf16[2,4,4,16,1536]{4,3,2,1,0:T(8,128)(2,1)} %get-tuple-element.13) | copy-start | bytes 4718596
where the time goes:
time: 135 us; the launch traced here: 134 us
  Pallas kernels  125 us (93%)
  local copies, waits for them, and re-layouts  5.42 us (4%)
  other arithmetic  1.65 us (1%)
    pallas_call x1, Pallas kernels, run_block(): pl.pallas_call(block_kernel, out_shape=[jax.ShapeDtypeStruct((256, 1536),...  125 us
    unnamed x5, local copies, waits for them, and re-layouts  4.57 us

commit v1 on v0

--- a/solution.py
+++ b/solution.py
@@ -23,9 +23,8 @@
     def __init__(self, send, recv):
         self.send, self.recv, self.made = send, recv, []
 
-    def start(self, src, dst, device):
-        index = len(self.made)
-        made = pltpu.make_async_remote_copy(
+    def make(self, src, dst, device, index):
+        return pltpu.make_async_remote_copy(
             src_ref=src,
             dst_ref=dst,
             send_sem=self.send.at[index],
@@ -33,13 +32,68 @@
             device_id=device,
             device_id_type=pl.DeviceIdType.MESH,
         )
+
+    def reserve(self, src, dst, device):
+        self.made.append(self.make(src, dst, device, len(self.made)))
+        return self.made[-1]
+
+    def start(self, src, dst, device):
+        made = self.reserve(src, dst, device)
         made.start()
-        self.made.append(made)
         return made
 
     def drain(self):
         for made in self.made:
             made.wait_send()
+
+
+class RowSwap:
+    def __init__(self, copies, relay_sems, spot, up, down, relay):
+        self.x, next_row, last_row, x_after, x_before, high_after, high_before = spot
+        self.relay = relay
+        index = len(copies.made)
+        self.up = copies.reserve(*up, next_row)
+        self.down = copies.reserve(*down, last_row)
+        self.waits = (self.up, self.down)
+        if relay is None:
+            self.up.start()
+            self.down.start()
+            return
+        self.up_forward = copies.make(relay, up[1], x_after, index)
+        self.down_forward = copies.make(relay, down[1], x_before, index + 1)
+        self.up_relay, self.down_relay = (
+            pltpu.make_async_remote_copy(
+                src_ref=src,
+                dst_ref=relay,
+                send_sem=relay_sems.at[0],
+                recv_sem=relay_sems.at[1],
+                device_id=device,
+                device_id_type=pl.DeviceIdType.MESH,
+            )
+            for src, device in ((up[0], high_after), (down[0], high_before))
+        )
+        for edge, direct, relayed in ((3, self.up, self.up_relay), (0, self.down, self.down_relay)):
+            pl.when(self.x == edge)(relayed.start)
+            pl.when(self.x != edge)(direct.start)
+
+    def forward(self):
+        for edge, relayed, onward in (
+            (3, self.up_relay, self.up_forward),
+            (0, self.down_relay, self.down_forward),
+        ):
+
+            @pl.when(self.x == edge)
+            def _():
+                relayed.wait_recv()
+                onward.start()
+
+    def wait(self):
+        for made in self.waits:
+            made.wait_recv()
+
+    def drain(self):
+        for edge, relayed in ((3, self.up_relay), (0, self.down_relay)):
+            pl.when(self.x == edge)(relayed.wait_send)
 
 
 class RingSum:
@@ -129,13 +183,14 @@
         need[f * 96 : f * 96 + 96] = base | jnp.where(outside, 8, time_gap)
 
 
-def block_kernel(q, kv_in, up, weight_in, windows, dq, dkv_out, fin, *refs):
+def block_kernel(q, kv_in, up, weight_in, windows, pick, dq, dkv_out, owned, *refs):
     f32, bf16 = jnp.float32, jnp.bfloat16
     kv, dkv, weight, probs_all, need, at, at_in, up_in = refs[:8]
     from_left, from_right, from_above, from_below = refs[8:12]
-    first_a, first_b, second_a, second_b, pair_sums, pair_in, tall, tall_in = refs[12:20]
-    rings = [refs[20 + 5 * i : 25 + 5 * i] for i in range(4)]
-    send, recv, local_sem = refs[40:]
+    first_a, first_b, second_a, second_b, pair_sums, pair_in, tall, tall_out, tall_in = refs[12:21]
+    last_out, last_in, relay_kv, relay_grad = refs[21:25]
+    rings = [refs[25 + 5 * i : 30 + 5 * i] for i in range(4)]
+    send, recv, relay_sems, local_sem = refs[45:]
     z_lo, y, core, z_hi, x = place()
     ta, ha = lax.axis_index("ta"), lax.axis_index("ha")
     partner = at_place(z_lo, y, 1 - core, z_hi, x)
@@ -146,6 +201,7 @@
     high_peers = [at_place(z_lo, y, core, (z_hi + s) % 4, x) for s in (1, 2, 3)]
     next_row, last_row = ({"ta": ta, "ha": (ha + s) % 16} for s in (1, 15))
     next_frame, last_frame = ({"ta": (ta + s) % 16, "ha": ha} for s in (1, 15))
+    spot = (x, next_row, last_row, x_after, x_before, high_peers[0], high_peers[2])
 
     own_copy = pltpu.make_async_copy(kv_in, kv.at[:, pl.ds(1, 4), pl.ds(1, 4)], local_sem)
     own_copy.start()
@@ -160,42 +216,68 @@
     copies = Copies(send, recv)
     start = copies.start
     mine = pl.ds(1, 4)
+    half_rows = pl.ds(pl.multiple_of(core * 48, 16), 48)
+    shared = pl.ds(0, 1024)
+    direct = pl.ds(1024, 512)
+
+    def quarter(p):
+        return pl.ds(pl.multiple_of(p * 256, 256), 256)
+
+    pieces_in = []
+    for cols in (quarter(y), direct):
+        piece = weight_in.at[half_rows, cols]
+        pieces_in.append([start(piece, weight.at[z_hi, x, core, :, cols], peer) for peer in high_peers])
+    near, far = pl.ds(0, 896), pl.ds(896, 640)
     rows_in = [
-        start(kv_in.at[:, :, 3], kv.at[:, mine, 0], next_row),
-        start(kv_in.at[:, :, 0], kv.at[:, mine, 5], last_row),
+        RowSwap(
+            copies,
+            relay_sems.at[i],
+            spot,
+            (kv_in.at[:, :, 3, :, cols], kv.at[:, mine, 0, :, cols]),
+            (kv_in.at[:, :, 0, :, cols], kv.at[:, mine, 5, :, cols]),
+            relay,
+        )
+        for i, (cols, relay) in enumerate(((far, relay_kv), (near, None)))
     ]
     frames_in = [
         start(kv_in.at[:, 3], kv.at[:, 0, mine], next_frame),
         start(kv_in.at[:, 0], kv.at[:, 5, mine], last_frame),
     ]
-    quarter = pl.ds(pl.multiple_of(y * 384, 384), 384)
-    piece = weight_in.at[pl.ds(pl.multiple_of(core * 48, 16), 48), quarter]
-    weight[z_hi, x, core, :, quarter] = weight_in[pl.ds(pl.multiple_of(core * 48, 16), 48), quarter]
-    pieces_in = [start(piece, weight.at[z_hi, x, core, :, quarter], peer) for peer in high_peers]
     up_swap = start(up, up_in, partner)
+    weight[z_hi, x, core, :, quarter(y)] = weight_in[half_rows, quarter(y)]
+    weight[z_hi, x, core, :, direct] = weight_in[half_rows, direct]
 
     def over_x(p, begin, size):
-        return weight.at[pl.ds(begin, size), p, core, :, quarter]
+        return weight.at[pl.ds(begin, size), p, core, :, quarter(y)]
+
+    def over_x_direct(p, begin, size):
+        return weight.at[pl.ds(begin, size), p, core, :, direct]
 
     def over_y(p, begin, size):
-        return weight.at[pl.ds(begin, size), :, core, :, pl.ds(pl.multiple_of(p * 384, 384), 384)]
+        return weight.at[pl.ds(begin, size), :, core, :, quarter(p)]
 
     gather_x = RingGather(copies, over_x, x, x_after, x_before)
+    gather_d = RingGather(copies, over_x_direct, x, x_after, x_before)
     gather_y = RingGather(copies, over_y, y, y_after, y_before)
-    for made in pieces_in:
+    for made in pieces_in[0]:
         made.wait_recv()
     gather_x.start()
-    for made in rows_in:
+    for made in pieces_in[1]:
         made.wait_recv()
+    gather_d.start()
+    gather_x.middle()
+    rows_in[0].forward()
+    gather_x.end()
+    gather_y.start()
+    swaps = [start(over_y(y, 0, 4), over_y(y, 0, 4), partner)]
+    for swap in rows_in:
+        swap.wait()
+    own_copy.wait()
     corners_in = []
     for frame, goal, device in ((4, 0, next_frame), (1, 5, last_frame)):
         for row in (0, 5):
             corners_in.append(start(kv.at[:, frame, row], kv.at[:, goal, row], device))
-    gather_x.middle()
-    gather_x.end()
-    gather_y.start()
-    swaps = [start(over_y(y, 0, 4), over_y(y, 0, 4), partner)]
-    own_copy.wait()
+    gather_d.middle()
     for made in (*frames_in, *corners_in):
         made.wait_recv()
 
@@ -248,12 +330,19 @@
             dkv[1, :, :, :, cols] = grad_values.reshape(6, 6, 16, 128)
         return carry
 
-    lax.fori_loop(0, 6, forward, 0)
-    at_swap = start(at.at[pl.ds((1 - core) * 8, 8)], at_in, partner)
+    lax.fori_loop(0, 3, forward, 0)
     gather_y.middle()
     for step in (3, 1):
         part = over_y((y + step) % 4, 0, 4)
         swaps.append(start(part, part, partner))
+    gather_d.end()
+    part = weight.at[:, :, core, :, direct]
+    swaps.append(start(part, part, partner))
+    lax.fori_loop(3, 6, forward, 0)
+    at_swap = start(at.at[pl.ds((1 - core) * 8, 8)], at_in, partner)
+    gather_y.end()
+    part = over_y((y + 2) % 4, 0, 4)
+    swaps.append(start(part, part, partner))
     up_swap.wait_recv()
     at_swap.wait_recv()
 
@@ -278,25 +367,43 @@
         for goal in range(4):
             first_a[goal, half] = block[goal * 96 : goal * 96 + 96]
     ring_a.start()
-    gather_y.end()
-    part = over_y((y + 2) % 4, 0, 4)
-    swaps.append(start(part, part, partner))
     for made in swaps:
         made.wait_recv()
     weight_rows = weight.reshape(1536, 1536)
+    inner, outer = pl.ds(2, 2), pl.ds(1, 2)
+
+    def frames_out(half):
+        cols = pl.ds(half * 768, 768)
+        sides = (
+            start(dkv.at[:, 5, :, :, cols], from_left.at[:, :, :, cols], next_frame),
+            start(dkv.at[:, 0, :, :, cols], from_right.at[:, :, :, cols], last_frame),
+        )
+        rows = RowSwap(
+            copies,
+            relay_sems.at[2 + half],
+            spot,
+            (dkv.at[:, inner, 5, :, cols], from_above.at[:, outer, :, cols]),
+            (dkv.at[:, inner, 0, :, cols], from_below.at[:, outer, :, cols]),
+            relay_grad.at[half],
+        )
+        return sides, rows
+
+    def rows_out(half, sides):
+        cols = pl.ds(half * 768, 768)
+        made = []
+        for side, frame, came, goal in ((sides[0], 1, from_left, 0), (sides[1], 4, from_right, 3)):
+            side.wait_recv()
+            total = dkv[:, frame, :, :, cols].astype(f32) + came[:, :, :, cols].astype(f32)
+            came[:, :, :, cols] = total.astype(bf16)
+            made.append(start(came.at[:, 5, :, cols], from_above.at[:, goal, :, cols], next_row))
+            made.append(start(came.at[:, 0, :, cols], from_below.at[:, goal, :, cols], last_row))
+        return made
+
     lax.fori_loop(0, 3, backward, 0)
+    sides_0, inner_0 = frames_out(0)
     ring_b.middle()
     ring_a.middle()
-    lax.fori_loop(3, 6, backward, 0)
-    sides = [
-        start(dkv.at[:, 5], from_left, next_frame),
-        start(dkv.at[:, 0], from_right, last_frame),
-    ]
-    inner = pl.ds(1, 2)
-    outer = [
-        start(dkv.at[:, pl.ds(2, 2), 5], from_above.at[:, inner], next_row),
-        start(dkv.at[:, pl.ds(2, 2), 0], from_below.at[:, inner], last_row),
-    ]
+    lax.fori_loop(3, 5, backward, 0)
     for half in range(2):
         block = ring_b.end(half).astype(bf16)
         for goal in range(2):
@@ -310,47 +417,60 @@
             for row in range(2):
                 second_a[half * 2 + goal, row] = block[row * 48 : row * 48 + 48, goal * 384 : goal * 384 + 384]
     ring_c.start()
-    for made, frame, came, first in ((sides[0], 1, from_left, 0), (sides[1], 4, from_right, 3)):
-        made.wait_recv()
-        for i in range(2):
-            total = dkv[i, frame].astype(f32) + came[i].astype(f32)
-            came[i] = total.astype(bf16)
-        outer.append(start(came.at[:, 5], from_above.at[:, first], next_row))
-        outer.append(start(came.at[:, 0], from_below.at[:, first], last_row))
+    lax.fori_loop(5, 6, backward, 0)
+    sides_1, inner_1 = frames_out(1)
+    outer_out = rows_out(0, sides_0)
     ring_d.middle()
     ring_c.middle()
+    inner_0.forward()
     for part, ring in ((1, ring_d), (0, ring_c)):
         for row in range(2):
             pair_sums[part, row * 48 : row * 48 + 48] = ring.end(row).astype(bf16)
     low = start(pair_sums.at[1 - z_lo], pair_in, low_peer)
+    outer_out += rows_out(1, sides_1)
     low.wait_recv()
     total = pair_sums[z_lo].astype(f32) + pair_in[...].astype(f32)
     tall[...] = total.astype(bf16)
-    highs = [start(tall, tall_in.at[i], high_peers[i]) for i in range(3)]
+    highs = []
+    for i in range(3):
+        chosen = pick[pl.ds(pl.multiple_of((z_hi + i + 1) % 4 * 48, 16), 48), :]
+        tall_out[i] = jnp.dot(chosen, tall[...], preferred_element_type=f32).astype(bf16)
+        highs.append(start(tall_out.at[i], tall_in.at[i], high_peers[i]))
+    inner_1.forward()
     for i in range(2):
         dkv_out[i, :, 1:3] = dkv[i, 1:5, 2:4]
-        for f in (1, 2):
-            for r in (0, 3):
-                dkv_out[i, f, r] = dkv[i, f + 1, r + 1]
         for f, came in ((0, from_left), (3, from_right)):
-            dkv_out[i, f] = came[i, 1:5]
-    for made in outer:
-        made.wait_recv()
-    for i in range(2):
-        for f in range(4):
-            for r, came in ((0, from_above), (3, from_below)):
-                dkv_out[i, f, r] = (dkv_out[i, f, r].astype(f32) + came[i, f].astype(f32)).astype(bf16)
+            dkv_out[i, f, 1:3] = came[i, 2:4]
+    chosen = pick[pl.ds(pl.multiple_of(z_hi * 48, 16), 48), :]
+    total = jnp.dot(chosen, tall[...], preferred_element_type=f32)
     for i in range(3):
         highs[i].wait_recv()
         total += tall_in[i].astype(f32)
-    fin[x] = (total * 0.00390625).astype(bf16)
-    lasts = [start(fin.at[x], fin.at[x], peer) for peer in x_peers]
+    total = total * 0.00390625
+    for goal in range(4):
+        last_out[goal, 0:12] = total[goal * 12 : goal * 12 + 12]
+        last_out[goal, 12:16] = jnp.zeros((4, 384), f32)
+    lasts = [start(last_out.at[(x + i + 1) % 4], last_in.at[x], x_peers[i]) for i in range(3)]
+    last_in[x] = last_out[x]
+    inner_0.wait()
+    inner_1.wait()
+    for made in outer_out:
+        made.wait_recv()
+    for i in range(2):
+        for f, own in ((0, from_left), (1, None), (2, None), (3, from_right)):
+            for r, came in ((0, from_above), (3, from_below)):
+                base = dkv[i, f + 1, r + 1] if own is None else own[i, r + 1]
+                dkv_out[i, f, r] = (base.astype(f32) + came[i, f].astype(f32)).astype(bf16)
     for made in lasts:
         made.wait_recv()
+    for goal in range(4):
+        owned[:, goal * 384 : goal * 384 + 384] = last_in[goal, 0:12]
     copies.drain()
-
-
-def run_block(q, kv, up, weight, windows):
+    for swap in (rows_in[0], inner_0, inner_1):
+        swap.drain()
+
+
+def run_block(q, kv, up, weight, windows, pick):
     bf16 = jnp.bfloat16
     vmem = pl.BlockSpec(memory_space=pltpu.VMEM)
     return pl.pallas_call(
@@ -358,9 +478,9 @@
         out_shape=[
             jax.ShapeDtypeStruct((256, 1536), bf16),
             jax.ShapeDtypeStruct((2, 4, 4, 16, 1536), bf16),
-            jax.ShapeDtypeStruct((4, 96, 384), bf16),
+            jax.ShapeDtypeStruct((12, 1536), jnp.float32),
         ],
-        in_specs=[vmem, pl.BlockSpec(memory_space=pl.ANY), vmem, vmem, pl.BlockSpec(memory_space=pltpu.SMEM)],
+        in_specs=[vmem, pl.BlockSpec(memory_space=pl.ANY), vmem, vmem, pl.BlockSpec(memory_space=pltpu.SMEM), vmem],
         out_specs=[vmem, vmem, vmem],
         scratch_shapes=[
             pltpu.VMEM((2, 6, 6, 16, 1536), bf16),
@@ -382,38 +502,46 @@
             pltpu.VMEM((2, 96, 384), bf16),
             pltpu.VMEM((96, 384), bf16),
             pltpu.VMEM((96, 384), bf16),
-            pltpu.VMEM((3, 96, 384), bf16),
+            pltpu.VMEM((3, 48, 384), bf16),
+            pltpu.VMEM((3, 48, 384), bf16),
+            pltpu.VMEM((4, 16, 384), jnp.float32),
+            pltpu.VMEM((4, 16, 384), jnp.float32),
+            pltpu.VMEM((2, 4, 16, 640), bf16),
+            pltpu.VMEM((2, 2, 2, 16, 768), bf16),
             *ring_buffers(96, 768),
             *ring_buffers(192, 384),
             *ring_buffers(48, 384),
             *ring_buffers(48, 384),
-            pltpu.SemaphoreType.DMA((64,)),
-            pltpu.SemaphoreType.DMA((64,)),
+            pltpu.SemaphoreType.DMA((90,)),
+            pltpu.SemaphoreType.DMA((90,)),
+            pltpu.SemaphoreType.DMA((4, 2)),
             pltpu.SemaphoreType.DMA,
         ],
         compiler_params=pltpu.CompilerParams(
             collective_id=1, has_side_effects=True, vmem_limit_bytes=56 * 1024 * 1024
         ),
-    )(q, kv, up, weight, windows)
-
-
-def owned_slots(fin, bucket_owner, height_index):
+    )(q, kv, up, weight, windows, pick)
+
+
+def slot_picks(bucket_owner):
     bucket_ids = jnp.arange(48, dtype=jnp.int32)
     same_owner = bucket_owner[None, :] == bucket_owner[:, None]
     ranking = jnp.sum((same_owner & (bucket_ids[None, :] < bucket_ids[:, None])).astype(jnp.int32), axis=1)
-    slot = jnp.where(bucket_owner == height_index, ranking, -1)
+    slot = bucket_owner * 6 + ranking
     chosen = jnp.repeat(slot * 2, 2) + jnp.tile(jnp.arange(2, dtype=jnp.int32), 48)
-    pick = (chosen[None, :] == jnp.arange(12, dtype=jnp.int32)[:, None]).astype(jnp.bfloat16)
-    owned = jnp.einsum("sr,xrc->sxc", pick, fin, preferred_element_type=jnp.float32)
-    return owned.reshape(6, 2, 1536)
+    return (chosen[None, :] == jnp.arange(192, dtype=jnp.int32)[:, None]).astype(jnp.bfloat16)
 
 
 def per_device(queries, keys_values, upstream, out_weight, windows, bucket_owner):
-    grad_query, grad_pairs, fin = run_block(
-        queries.reshape(256, 1536), keys_values, upstream.reshape(256, 1536), out_weight, windows
+    grad_query, grad_pairs, owned = run_block(
+        queries.reshape(256, 1536),
+        keys_values,
+        upstream.reshape(256, 1536),
+        out_weight,
+        windows,
+        slot_picks(bucket_owner),
     )
-    owned = owned_slots(fin, bucket_owner, lax.axis_index("ha"))
-    return grad_query.reshape(queries.shape), grad_pairs, owned
+    return grad_query.reshape(queries.shape), grad_pairs, owned.reshape(6, 2, 1536)
 
 
 def solution(mesh):

time: 135 us -> 112 us (0.83)
  Pallas kernels: 125 us -> 102 us
    pallas_call x1, Pallas kernels: 125 us -> 102 us  [run_block(): pl.pallas_call(block_kernel, out_shape=[jax.ShapeDtypeStruct((256, 1536),...]
where the time goes in v1:
time: 112 us
  Pallas kernels  102 us (91%)
  local copies, waits for them, and re-layouts  6.38 us (6%)
  other arithmetic  2.29 us (2%)
    pallas_call x1, Pallas kernels, run_block(): pl.pallas_call(block_kernel, out_shape=[jax.ShapeDtypeStruct((256, 1536),...  102 us
    unnamed x5, local copies, waits for them, and re-layouts  4.57 us

profile of v1, /device:TPU:6, one launch (start us, length us, event | category | flops | bytes accessed | tf_op | source)
XLA Modules:
  0.0 111.7 jit_solution(2656210519154352762)
XLA Ops:
  0.6 0.9 convert_reduce_fusion
  1.5 0.7 add_multiply_fusion
  2.2 1.4 %copy.11.windows = s32[12,3]{1,0:T(8,128)} copy(s32[12,3]{0,1:T(4,128)} %param.10) | data formatting | bytes 288 | tf_op args[4]
  3.6 0.1 iota_add_fusion
  3.6 0.1 add.15
  3.8 0.6 fusion.pick
  4.4 102.4 %shard_map.85 = (bf16[256,1536]{1,0:T(8,128)(2,1)}, bf16[2,4,4,16,1536]{4,3,2,1,0:T(8,128)(2,1)}, f32[12,1536]{1,0:T(8,128)}) custom-call(bf16[256,1536]{1,0:T(8,128)(2,1)} %bitcast.4, bf16[2,4,4,16,1536]{4,3,2,1,0:T(8,128)(2,1)} %kv_in.1, bf16[256,1536]{1,0:T(8,128)(2,1)} %bitcast.5, bf16[96,1536]{1,0:T(8,128)(2,1)} %weight_in.1, s32[12,3]{1,0:T(8,128)} %copy.11.windows, ...), custom_call_target="tpu_custom_call" | custom-call | tf_op jit(solution)/shard_map/pallas_call | solution.py:476
  106.8 0.0 copy-start
  106.8 1.7 %reshape.34 = f32[6,2,1536]{2,1,0:T(2,128)} reshape(f32[12,1536]{1,0:T(8,128)} %get-tuple-element.8) | data formatting | bytes 147456 | tf_op jit(solution)/shard_map/reshape | solution.py:544
  108.5 2.1 %copy.14 = bf16[4,4,16,1536]{3,2,1,0:T(8,128)(2,1)} copy(bf16[4,4,16,1536]{3,2,1,0:T(8,128)(2,1)} %bitcast.3) | data formatting | bytes 1572864
  110.5 0.0 copy-done
  110.5 1.1 %copy.15 = bf16[2,4,4,16,1536]{4,3,2,1,0:T(8,128)(2,1)} copy(bf16[2,4,4,16,1536]{4,3,2,1,0:T(8,128)(2,1)S(1)} %copy-done) | data formatting | bytes 3145728
Async XLA Ops:
  106.8 3.8 %copy-start = (bf16[2,4,4,16,1536]{4,3,2,1,0:T(8,128)(2,1)S(1)}, bf16[2,4,4,16,1536]{4,3,2,1,0:T(8,128)(2,1)}, u32[]{:S(2)}) copy-start(bf16[2,4,4,16,1536]{4,3,2,1,0:T(8,128)(2,1)} %get-tuple-element.13) | copy-start | bytes 4718596

commit v2 on v1

--- a/solution.py
+++ b/solution.py
@@ -21,25 +21,23 @@
 
 class Copies:
     def __init__(self, send, recv):
-        self.send, self.recv, self.made = send, recv, []
-
-    def make(self, src, dst, device, index):
+        self.send, self.recv, self.made, self.count = send, recv, [], 0
+
+    def make(self, src, dst, device, send=None, recv=None):
+        self.count += recv is None
         return pltpu.make_async_remote_copy(
             src_ref=src,
             dst_ref=dst,
-            send_sem=self.send.at[index],
-            recv_sem=self.recv.at[index],
+            send_sem=self.send.at[self.count - 1] if send is None else send,
+            recv_sem=self.recv.at[self.count - 1] if recv is None else recv,
             device_id=device,
             device_id_type=pl.DeviceIdType.MESH,
         )
 
-    def reserve(self, src, dst, device):
-        self.made.append(self.make(src, dst, device, len(self.made)))
-        return self.made[-1]
-
     def start(self, src, dst, device):
-        made = self.reserve(src, dst, device)
+        made = self.make(src, dst, device)
         made.start()
+        self.made.append(made)
         return made
 
     def drain(self):
@@ -50,36 +48,25 @@
 class RowSwap:
     def __init__(self, copies, relay_sems, spot, up, down, relay):
         self.x, next_row, last_row, x_after, x_before, high_after, high_before = spot
-        self.relay = relay
-        index = len(copies.made)
-        self.up = copies.reserve(*up, next_row)
-        self.down = copies.reserve(*down, last_row)
-        self.waits = (self.up, self.down)
-        if relay is None:
-            self.up.start()
-            self.down.start()
+        self.relayed = relay is not None
+        if not self.relayed:
+            self.up, self.down = copies.start(*up, next_row), copies.start(*down, last_row)
             return
-        self.up_forward = copies.make(relay, up[1], x_after, index)
-        self.down_forward = copies.make(relay, down[1], x_before, index + 1)
-        self.up_relay, self.down_relay = (
-            pltpu.make_async_remote_copy(
-                src_ref=src,
-                dst_ref=relay,
-                send_sem=relay_sems.at[0],
-                recv_sem=relay_sems.at[1],
-                device_id=device,
-                device_id_type=pl.DeviceIdType.MESH,
-            )
-            for src, device in ((up[0], high_after), (down[0], high_before))
-        )
+        self.up, self.down = copies.make(*up, next_row), copies.make(*down, last_row)
+        out, back, onward = (relay_sems.at[i] for i in range(3))
+        recv = copies.count - 2
+        self.up_relay = copies.make(up[0], relay, x_after, out, back)
+        self.down_relay = copies.make(down[0], relay, x_before, out, back)
+        self.up_forward = copies.make(relay, up[1], high_after, onward, copies.recv.at[recv])
+        self.down_forward = copies.make(relay, down[1], high_before, onward, copies.recv.at[recv + 1])
         for edge, direct, relayed in ((3, self.up, self.up_relay), (0, self.down, self.down_relay)):
             pl.when(self.x == edge)(relayed.start)
             pl.when(self.x != edge)(direct.start)
 
     def forward(self):
         for edge, relayed, onward in (
-            (3, self.up_relay, self.up_forward),
-            (0, self.down_relay, self.down_forward),
+            (0, self.up_relay, self.up_forward),
+            (3, self.down_relay, self.down_forward),
         ):
 
             @pl.when(self.x == edge)
@@ -88,12 +75,19 @@
                 onward.start()
 
     def wait(self):
-        for made in self.waits:
-            made.wait_recv()
+        self.up.wait_recv()
+        self.down.wait_recv()
 
     def drain(self):
-        for edge, relayed in ((3, self.up_relay), (0, self.down_relay)):
-            pl.when(self.x == edge)(relayed.wait_send)
+        pl.when(self.x != 3)(self.up.wait_send)
+        pl.when(self.x != 0)(self.down.wait_send)
+        for edge, made in (
+            (3, self.up_relay),
+            (0, self.down_relay),
+            (0, self.up_forward),
+            (3, self.down_forward),
+        ):
+            pl.when(self.x == edge)(made.wait_send)
 
 
 class RingSum:
@@ -183,14 +177,39 @@
         need[f * 96 : f * 96 + 96] = base | jnp.where(outside, 8, time_gap)
 
 
-def block_kernel(q, kv_in, up, weight_in, windows, pick, dq, dkv_out, owned, *refs):
+def window_blocks(windows, blocks):
+    axis = lax.broadcasted_iota(jnp.int32, (3, HEADS), 0)
+    bits = jnp.sum(jnp.where(windows[...] > 1, 1 << axis, 0), axis=0, keepdims=True)
+    row = lax.broadcasted_iota(jnp.int32, (HEADS, HEADS), 0)
+    lane = lax.broadcasted_iota(jnp.int32, (HEADS, HEADS), 1)
+    down = jnp.sum(jnp.where(row == lane, bits, 0), axis=1, keepdims=True)
+    blocks[...] = jnp.broadcast_to(15 - down, (HEADS, 256))
+
+
+def slot_picks(bucket_owner, pick):
+    owners = bucket_owner[...].reshape(1, 48)
+    row = lax.broadcasted_iota(jnp.int32, (48, 48), 0)
+    lane = lax.broadcasted_iota(jnp.int32, (48, 48), 1)
+    down = jnp.sum(jnp.where(row == lane, owners, 0), axis=1, keepdims=True)
+    row = lax.broadcasted_iota(jnp.int32, (48, 96), 0)
+    lane = lax.broadcasted_iota(jnp.int32, (48, 96), 1)
+    along = jnp.sum(jnp.where(row == lane >> 1, down, 0), axis=0, keepdims=True)
+    earlier = (down == along) & (row < lane >> 1)
+    ranking = jnp.sum(jnp.where(earlier, 1, 0), axis=0, keepdims=True)
+    chosen = along * 12 + ranking * 2 + (lane[0:1] & 1)
+    row = lax.broadcasted_iota(jnp.int32, (192, 96), 0)
+    pick[...] = jnp.where(row == chosen, 1.0, 0.0).astype(jnp.bfloat16)
+
+
+def block_kernel(q_in, kv_in, up_hbm, weight_in, windows, bucket_owner, dq_out, dkv_hbm, owned, *refs):
     f32, bf16 = jnp.float32, jnp.bfloat16
     kv, dkv, weight, probs_all, need, at, at_in, up_in = refs[:8]
     from_left, from_right, from_above, from_below = refs[8:12]
     first_a, first_b, second_a, second_b, pair_sums, pair_in, tall, tall_out, tall_in = refs[12:21]
     last_out, last_in, relay_kv, relay_grad = refs[21:25]
     rings = [refs[25 + 5 * i : 30 + 5 * i] for i in range(4)]
-    send, recv, relay_sems, local_sem = refs[45:]
+    q, up, dq, dkv_out, pick, blocks = refs[45:51]
+    send, recv, relay_sems, local_sem = refs[51:]
     z_lo, y, core, z_hi, x = place()
     ta, ha = lax.axis_index("ta"), lax.axis_index("ha")
     partner = at_place(z_lo, y, 1 - core, z_hi, x)
@@ -203,30 +222,55 @@
     next_frame, last_frame = ({"ta": (ta + s) % 16, "ha": ha} for s in (1, 15))
     spot = (x, next_row, last_row, x_after, x_before, high_peers[0], high_peers[2])
 
-    own_copy = pltpu.make_async_copy(kv_in, kv.at[:, pl.ds(1, 4), pl.ds(1, 4)], local_sem)
-    own_copy.start()
+    own_copies = [
+        pltpu.make_async_copy(src, dst, local_sem.at[i])
+        for i, (src, dst) in enumerate(((kv_in, kv.at[:, pl.ds(1, 4), pl.ds(1, 4)]), (q_in, q), (up_hbm, up)))
+    ]
+    half_rows = pl.ds(pl.multiple_of(core * 48, 16), 48)
+    shared = pl.ds(pl.multiple_of(y * 256, 256), 256)
+    direct = pl.ds(1024, 512)
+    own_copies += [
+        pltpu.make_async_copy(
+            weight_in.at[half_rows, cols], weight.at[z_hi, x, core, :, cols], local_sem.at[3 + i]
+        )
+        for i, cols in enumerate((shared, direct))
+    ]
+    for made in own_copies:
+        made.start()
     peers = [partner, y_after, y_before, *x_peers, low_peer, *high_peers]
     peers += [next_row, last_row, next_frame, last_frame]
     barrier = pltpu.get_barrier_semaphore()
     for peer in peers:
         pl.semaphore_signal(barrier, inc=1, device_id=peer, device_id_type=pl.DeviceIdType.MESH)
     window_bits(need)
+    window_blocks(windows, blocks)
+    slot_picks(bucket_owner, pick)
     pl.semaphore_wait(barrier, len(peers))
 
     copies = Copies(send, recv)
     start = copies.start
     mine = pl.ds(1, 4)
-    half_rows = pl.ds(pl.multiple_of(core * 48, 16), 48)
-    shared = pl.ds(0, 1024)
-    direct = pl.ds(1024, 512)
 
     def quarter(p):
         return pl.ds(pl.multiple_of(p * 256, 256), 256)
 
-    pieces_in = []
-    for cols in (quarter(y), direct):
+    def pieces(cols):
         piece = weight_in.at[half_rows, cols]
-        pieces_in.append([start(piece, weight.at[z_hi, x, core, :, cols], peer) for peer in high_peers])
+        return [start(piece, weight.at[z_hi, x, core, :, cols], peer) for peer in high_peers]
+
+    def over_x(p, begin, size):
+        return weight.at[pl.ds(begin, size), p, core, :, quarter(y)]
+
+    def over_x_direct(p, begin, size):
+        return weight.at[pl.ds(begin, size), p, core, :, direct]
+
+    def over_y(p, begin, size):
+        return weight.at[pl.ds(begin, size), :, core, :, quarter(p)]
+
+    gather_x = RingGather(copies, over_x, x, x_after, x_before)
+    gather_d = RingGather(copies, over_x_direct, x, x_after, x_before)
+    gather_y = RingGather(copies, over_y, y, y_after, y_before)
+    shared_in = pieces(shared)
     near, far = pl.ds(0, 896), pl.ds(896, 640)
     rows_in = [
         RowSwap(
@@ -243,41 +287,25 @@
         start(kv_in.at[:, 3], kv.at[:, 0, mine], next_frame),
         start(kv_in.at[:, 0], kv.at[:, 5, mine], last_frame),
     ]
-    up_swap = start(up, up_in, partner)
-    weight[z_hi, x, core, :, quarter(y)] = weight_in[half_rows, quarter(y)]
-    weight[z_hi, x, core, :, direct] = weight_in[half_rows, direct]
-
-    def over_x(p, begin, size):
-        return weight.at[pl.ds(begin, size), p, core, :, quarter(y)]
-
-    def over_x_direct(p, begin, size):
-        return weight.at[pl.ds(begin, size), p, core, :, direct]
-
-    def over_y(p, begin, size):
-        return weight.at[pl.ds(begin, size), :, core, :, quarter(p)]
-
-    gather_x = RingGather(copies, over_x, x, x_after, x_before)
-    gather_d = RingGather(copies, over_x_direct, x, x_after, x_before)
-    gather_y = RingGather(copies, over_y, y, y_after, y_before)
-    for made in pieces_in[0]:
+    up_swap = start(up_hbm, up_in, partner)
+    for made in shared_in:
         made.wait_recv()
+    own_copies[3].wait()
     gather_x.start()
-    for made in pieces_in[1]:
-        made.wait_recv()
-    gather_d.start()
     gather_x.middle()
     rows_in[0].forward()
-    gather_x.end()
-    gather_y.start()
-    swaps = [start(over_y(y, 0, 4), over_y(y, 0, 4), partner)]
     for swap in rows_in:
         swap.wait()
-    own_copy.wait()
+    for made in (*own_copies[:3], own_copies[4]):
+        made.wait()
     corners_in = []
     for frame, goal, device in ((4, 0, next_frame), (1, 5, last_frame)):
         for row in (0, 5):
             corners_in.append(start(kv.at[:, frame, row], kv.at[:, goal, row], device))
-    gather_d.middle()
+    direct_in = pieces(direct)
+    gather_x.end()
+    gather_y.start()
+    swaps = [start(over_y(y, 0, 4), over_y(y, 0, 4), partner)]
     for made in (*frames_in, *corners_in):
         made.wait_recv()
 
@@ -296,7 +324,7 @@
             head = pair * 2 + side
             cols = pl.ds(pl.multiple_of(head * 128, 128), 128)
             keys, values = (kv[i, :, :, :, cols].reshape(576, 128) for i in range(2))
-            block = 15 - sum(((windows[head, a] - 1) // 2) << a for a in range(3))
+            block = blocks[pl.ds(head, 1), :]
             scores = lax.dot_general(keys, q[:, cols], ACROSS, preferred_element_type=f32)
             scores = jnp.where((need[...] & block) == 0, scores, -1e30)
             highest = jnp.max(scores, axis=0, keepdims=True)
@@ -330,19 +358,17 @@
             dkv[1, :, :, :, cols] = grad_values.reshape(6, 6, 16, 128)
         return carry
 
+    for made in direct_in:
+        made.wait_recv()
+    gather_d.start()
     lax.fori_loop(0, 3, forward, 0)
     gather_y.middle()
     for step in (3, 1):
         part = over_y((y + step) % 4, 0, 4)
         swaps.append(start(part, part, partner))
-    gather_d.end()
-    part = weight.at[:, :, core, :, direct]
-    swaps.append(start(part, part, partner))
     lax.fori_loop(3, 6, forward, 0)
     at_swap = start(at.at[pl.ds((1 - core) * 8, 8)], at_in, partner)
-    gather_y.end()
-    part = over_y((y + 2) % 4, 0, 4)
-    swaps.append(start(part, part, partner))
+    gather_d.middle()
     up_swap.wait_recv()
     at_swap.wait_recv()
 
@@ -367,6 +393,12 @@
         for goal in range(4):
             first_a[goal, half] = block[goal * 96 : goal * 96 + 96]
     ring_a.start()
+    gather_d.end()
+    part = weight.at[:, :, core, :, direct]
+    swaps.append(start(part, part, partner))
+    gather_y.end()
+    part = over_y((y + 2) % 4, 0, 4)
+    swaps.append(start(part, part, partner))
     for made in swaps:
         made.wait_recv()
     weight_rows = weight.reshape(1536, 1536)
@@ -399,11 +431,12 @@
             made.append(start(came.at[:, 0, :, cols], from_below.at[:, goal, :, cols], last_row))
         return made
 
-    lax.fori_loop(0, 3, backward, 0)
-    sides_0, inner_0 = frames_out(0)
+    lax.fori_loop(0, 2, backward, 0)
     ring_b.middle()
     ring_a.middle()
-    lax.fori_loop(3, 5, backward, 0)
+    lax.fori_loop(2, 3, backward, 0)
+    sides_0, inner_0 = frames_out(0)
+    lax.fori_loop(3, 4, backward, 0)
     for half in range(2):
         block = ring_b.end(half).astype(bf16)
         for goal in range(2):
@@ -417,16 +450,19 @@
             for row in range(2):
                 second_a[half * 2 + goal, row] = block[row * 48 : row * 48 + 48, goal * 384 : goal * 384 + 384]
     ring_c.start()
-    lax.fori_loop(5, 6, backward, 0)
-    sides_1, inner_1 = frames_out(1)
+    lax.fori_loop(4, 5, backward, 0)
     outer_out = rows_out(0, sides_0)
     ring_d.middle()
     ring_c.middle()
-    inner_0.forward()
+    lax.fori_loop(5, 6, backward, 0)
+    sides_1, inner_1 = frames_out(1)
+    results = [pltpu.make_async_copy(dq, dq_out, local_sem.at[5])]
+    results[0].start()
     for part, ring in ((1, ring_d), (0, ring_c)):
         for row in range(2):
             pair_sums[part, row * 48 : row * 48 + 48] = ring.end(row).astype(bf16)
     low = start(pair_sums.at[1 - z_lo], pair_in, low_peer)
+    inner_0.forward()
     outer_out += rows_out(1, sides_1)
     low.wait_recv()
     total = pair_sums[z_lo].astype(f32) + pair_in[...].astype(f32)
@@ -441,6 +477,13 @@
         dkv_out[i, :, 1:3] = dkv[i, 1:5, 2:4]
         for f, came in ((0, from_left), (3, from_right)):
             dkv_out[i, f, 1:3] = came[i, 2:4]
+
+    def result(index, rows):
+        made = pltpu.make_async_copy(dkv_out.at[:, :, rows], dkv_hbm.at[:, :, rows], local_sem.at[index])
+        made.start()
+        results.append(made)
+
+    result(6, pl.ds(1, 2))
     chosen = pick[pl.ds(pl.multiple_of(z_hi * 48, 16), 48), :]
     total = jnp.dot(chosen, tall[...], preferred_element_type=f32)
     for i in range(3):
@@ -461,27 +504,33 @@
             for r, came in ((0, from_above), (3, from_below)):
                 base = dkv[i, f + 1, r + 1] if own is None else own[i, r + 1]
                 dkv_out[i, f, r] = (base.astype(f32) + came[i, f].astype(f32)).astype(bf16)
+    result(7, pl.ds(0, 1))
+    result(8, pl.ds(3, 1))
     for made in lasts:
         made.wait_recv()
     for goal in range(4):
-        owned[:, goal * 384 : goal * 384 + 384] = last_in[goal, 0:12]
+        for slot in range(6):
+            owned[slot, :, goal * 384 : goal * 384 + 384] = last_in[goal, slot * 2 : slot * 2 + 2]
+    for made in results:
+        made.wait()
     copies.drain()
     for swap in (rows_in[0], inner_0, inner_1):
         swap.drain()
 
 
-def run_block(q, kv, up, weight, windows, pick):
+def run_block(q, kv, up, weight, windows, bucket_owner):
     bf16 = jnp.bfloat16
     vmem = pl.BlockSpec(memory_space=pltpu.VMEM)
+    anywhere = pl.BlockSpec(memory_space=pl.ANY)
     return pl.pallas_call(
         block_kernel,
         out_shape=[
             jax.ShapeDtypeStruct((256, 1536), bf16),
             jax.ShapeDtypeStruct((2, 4, 4, 16, 1536), bf16),
-            jax.ShapeDtypeStruct((12, 1536), jnp.float32),
+            jax.ShapeDtypeStruct((6, 2, 1536), jnp.float32),
         ],
-        in_specs=[vmem, pl.BlockSpec(memory_space=pl.ANY), vmem, vmem, pl.BlockSpec(memory_space=pltpu.SMEM), vmem],
-        out_specs=[vmem, vmem, vmem],
+        in_specs=[anywhere, anywhere, anywhere, anywhere, vmem, vmem],
+        out_specs=[anywhere, anywhere, vmem],
         scratch_shapes=[
             pltpu.VMEM((2, 6, 6, 16, 1536), bf16),
             pltpu.VMEM((2, 6, 6, 16, 1536), bf16),
@@ -512,24 +561,21 @@
             *ring_buffers(192, 384),
             *ring_buffers(48, 384),
             *ring_buffers(48, 384),
+            pltpu.VMEM((256, 1536), bf16),
+            pltpu.VMEM((256, 1536), bf16),
+            pltpu.VMEM((256, 1536), bf16),
+            pltpu.VMEM((2, 4, 4, 16, 1536), bf16),
+            pltpu.VMEM((192, 96), bf16),
+            pltpu.VMEM((HEADS, 256), jnp.int32),
             pltpu.SemaphoreType.DMA((90,)),
             pltpu.SemaphoreType.DMA((90,)),
-            pltpu.SemaphoreType.DMA((4, 2)),
-            pltpu.SemaphoreType.DMA,
+            pltpu.SemaphoreType.DMA((4, 3)),
+            pltpu.SemaphoreType.DMA((9,)),
         ],
         compiler_params=pltpu.CompilerParams(
             collective_id=1, has_side_effects=True, vmem_limit_bytes=56 * 1024 * 1024
         ),
-    )(q, kv, up, weight, windows, pick)
-
-
-def slot_picks(bucket_owner):
-    bucket_ids = jnp.arange(48, dtype=jnp.int32)
-    same_owner = bucket_owner[None, :] == bucket_owner[:, None]
-    ranking = jnp.sum((same_owner & (bucket_ids[None, :] < bucket_ids[:, None])).astype(jnp.int32), axis=1)
-    slot = bucket_owner * 6 + ranking
-    chosen = jnp.repeat(slot * 2, 2) + jnp.tile(jnp.arange(2, dtype=jnp.int32), 48)
-    return (chosen[None, :] == jnp.arange(192, dtype=jnp.int32)[:, None]).astype(jnp.bfloat16)
+    )(q, kv, up, weight, windows, bucket_owner)
 
 
 def per_device(queries, keys_values, upstream, out_weight, windows, bucket_owner):
@@ -538,10 +584,10 @@
         keys_values,
         upstream.reshape(256, 1536),
         out_weight,
-        windows,
-        slot_picks(bucket_owner),
+        windows.T,
+        bucket_owner,
     )
-    return grad_query.reshape(queries.shape), grad_pairs, owned.reshape(6, 2, 1536)
+    return grad_query.reshape(queries.shape), grad_pairs, owned
 
 
 def solution(mesh):

time: 112 us -> 102 us (0.911); the launches traced: 112 us -> 99.9 us
  Pallas kernels: 102 us -> 95.3 us
  local copies, waits for them, and re-layouts: 6.38 us -> 3.96 us
  other arithmetic: 2.29 us -> 0 us
    pallas_call x1, Pallas kernels: 102 us -> 95.3 us  [run_block(): pl.pallas_call(block_kernel, out_shape=[jax.ShapeDtypeStruct((256, 1536),...]
    reshape x1 -> x0, local copies, waits for them, and re-layouts: 1.69 us -> none  [per_device(): owned.reshape(6, 2, 1536)]
    unnamed x5 -> x7, local copies, waits for them, and re-layouts: 4.57 us -> 3.96 us
where the time goes in v2:
time: 102 us; the launch traced here: 99.9 us
  Pallas kernels  95.3 us (93%)
  local copies, waits for them, and re-layouts  3.96 us (4%)
    pallas_call x1, Pallas kernels, run_block(): pl.pallas_call(block_kernel, out_shape=[jax.ShapeDtypeStruct((256, 1536),...  95.3 us
    unnamed x7, local copies, waits for them, and re-layouts  3.96 us

profile of v2, /device:TPU:6, one launch (start us, length us, event | category | flops | bytes accessed | tf_op | source)
XLA Modules:
  0.0 99.9 jit_solution(11418528128528023060)
XLA Ops:
  0.6 95.3 %shard_map.85 = (bf16[256,1536]{1,0:T(8,128)(2,1)}, bf16[2,4,4,16,1536]{4,3,2,1,0:T(8,128)(2,1)}, f32[6,2,1536]{2,1,0:T(2,128)}) custom-call(bf16[256,1536]{1,0:T(8,128)(2,1)} %bitcast.5, bf16[2,4,4,16,1536]{4,3,2,1,0:T(8,128)(2,1)} %kv_in.1, bf16[256,1536]{1,0:T(8,128)(2,1)} %bitcast.6, bf16[96,1536]{1,0:T(8,128)(2,1)} %weight_in.1, s32[3,12]{1,0:T(4,128)} %bitcast.7, ...), custom_call_target="tpu_custom_call" | custom-call | tf_op jit(solution)/shard_map/pallas_call | solution.py:525
  95.9 0.0 copy-start
  95.9 2.2 %copy.12 = bf16[4,4,16,1536]{3,2,1,0:T(8,128)(2,1)} copy(bf16[4,4,16,1536]{3,2,1,0:T(8,128)(2,1)} %bitcast.4) | data formatting | bytes 1572864
  98.1 0.0 copy-done
  98.1 0.0 copy-start.1
  98.1 1.1 %copy.13 = bf16[2,4,4,16,1536]{4,3,2,1,0:T(8,128)(2,1)} copy(bf16[2,4,4,16,1536]{4,3,2,1,0:T(8,128)(2,1)S(1)} %copy-done) | data formatting | bytes 3145728
  99.2 0.0 copy-done.1
  99.2 0.6 copy.14
Async XLA Ops:
  95.9 2.2 %copy-start = (bf16[2,4,4,16,1536]{4,3,2,1,0:T(8,128)(2,1)S(1)}, bf16[2,4,4,16,1536]{4,3,2,1,0:T(8,128)(2,1)}, u32[]{:S(2)}) copy-start(bf16[2,4,4,16,1536]{4,3,2,1,0:T(8,128)(2,1)} %get-tuple-element.13) | copy-start | bytes 4718596
  98.1 1.1 %copy-start.1 = (f32[6,2,1536]{2,1,0:T(2,128)S(1)}, f32[6,2,1536]{2,1,0:T(2,128)}, u32[]{:S(2)}) copy-start(f32[6,2,1536]{2,1,0:T(2,128)} %get-tuple-element.14) | copy-start | bytes 221188

commit v3 on v2

--- a/solution.py
+++ b/solution.py
@@ -7,6 +7,7 @@
 
 HEADS = 12
 HEAD_DIM = 128
+NEAR, FAR = 896, 640
 ACROSS = (((1,), (1,)), ((), ()))
 
 
@@ -130,6 +131,24 @@
         )
 
 
+class DirectSum:
+    def __init__(self, copies, src, pos, peers, came):
+        self.copies, self.src, self.pos, self.peers, self.came = copies, src, pos, peers, came
+
+    def start(self):
+        self.made = [
+            self.copies.start(self.src.at[(self.pos + i + 1) % 4], self.came.at[i], self.peers[i])
+            for i in range(3)
+        ]
+
+    def end(self):
+        total = self.src[self.pos].astype(jnp.float32)
+        for i in range(3):
+            self.made[i].wait_recv()
+            total += self.came[i].astype(jnp.float32)
+        return total
+
+
 def ring_buffers(rows, columns):
     return [
         pltpu.VMEM((2, rows, columns), jnp.bfloat16),
@@ -141,25 +160,28 @@
 
 
 class RingGather:
-    def __init__(self, copies, block, pos, after, before):
-        self.copies, self.block, self.pos, self.after, self.before = copies, block, pos, after, before
+    def __init__(self, copies, blocks, pos, after, before):
+        self.copies, self.blocks, self.pos, self.after, self.before = copies, blocks, pos, after, before
+
+    def send(self, step, begin, size, device):
+        parts = self.blocks((self.pos + step) % 4, begin, size)
+        return [self.copies.start(part, part, device) for part in parts]
 
     def start(self):
-        own = self.block(self.pos, 0, 4)
-        self.from_before = self.copies.start(own, own, self.after)
-        self.from_after = self.copies.start(own, own, self.before)
+        self.from_before = self.send(0, 0, 4, self.after)
+        self.from_after = self.send(0, 0, 4, self.before)
 
     def middle(self):
-        self.from_before.wait_recv()
-        part = self.block((self.pos + 3) % 4, 0, 2)
-        self.far_before = self.copies.start(part, part, self.after)
-        self.from_after.wait_recv()
-        part = self.block((self.pos + 1) % 4, 2, 2)
-        self.far_after = self.copies.start(part, part, self.before)
+        for made in self.from_before:
+            made.wait_recv()
+        self.far = self.send(3, 0, 2, self.after)
+        for made in self.from_after:
+            made.wait_recv()
+        self.far += self.send(1, 2, 2, self.before)
 
     def end(self):
-        self.far_before.wait_recv()
-        self.far_after.wait_recv()
+        for made in self.far:
+            made.wait_recv()
 
 
 def window_bits(need):
@@ -196,8 +218,8 @@
     along = jnp.sum(jnp.where(row == lane >> 1, down, 0), axis=0, keepdims=True)
     earlier = (down == along) & (row < lane >> 1)
     ranking = jnp.sum(jnp.where(earlier, 1, 0), axis=0, keepdims=True)
-    chosen = along * 12 + ranking * 2 + (lane[0:1] & 1)
-    row = lax.broadcasted_iota(jnp.int32, (192, 96), 0)
+    chosen = along * 16 + ranking * 2 + (lane[0:1] & 1)
+    row = lax.broadcasted_iota(jnp.int32, (256, 96), 0)
     pick[...] = jnp.where(row == chosen, 1.0, 0.0).astype(jnp.bfloat16)
 
 
@@ -205,11 +227,11 @@
     f32, bf16 = jnp.float32, jnp.bfloat16
     kv, dkv, weight, probs_all, need, at, at_in, up_in = refs[:8]
     from_left, from_right, from_above, from_below = refs[8:12]
-    first_a, first_b, second_a, second_b, pair_sums, pair_in, tall, tall_out, tall_in = refs[12:21]
-    last_out, last_in, relay_kv, relay_grad = refs[21:25]
-    rings = [refs[25 + 5 * i : 30 + 5 * i] for i in range(4)]
-    q, up, dq, dkv_out, pick, blocks = refs[45:51]
-    send, recv, relay_sems, local_sem = refs[51:]
+    first_a, first_b, second_a, second_b, came_a, came_b, pair_sums, pair_in = refs[12:20]
+    slots_out, slots_in, relay_kv, relay_grad = refs[20:24]
+    rings = [refs[24 + 5 * i : 29 + 5 * i] for i in range(2)]
+    q, up, dq, dkv_out, pick, blocks = refs[34:40]
+    send, recv, relay_sems, local_sem = refs[40:]
     z_lo, y, core, z_hi, x = place()
     ta, ha = lax.axis_index("ta"), lax.axis_index("ha")
     partner = at_place(z_lo, y, 1 - core, z_hi, x)
@@ -227,18 +249,19 @@
         for i, (src, dst) in enumerate(((kv_in, kv.at[:, pl.ds(1, 4), pl.ds(1, 4)]), (q_in, q), (up_hbm, up)))
     ]
     half_rows = pl.ds(pl.multiple_of(core * 48, 16), 48)
-    shared = pl.ds(pl.multiple_of(y * 256, 256), 256)
-    direct = pl.ds(1024, 512)
-    own_copies += [
-        pltpu.make_async_copy(
-            weight_in.at[half_rows, cols], weight.at[z_hi, x, core, :, cols], local_sem.at[3 + i]
-        )
-        for i, cols in enumerate((shared, direct))
+    tiles = [
+        pl.multiple_of(jnp.where(z_hi % 2 == 0, even, odd) * 128, 128)
+        for even, odd in ((y * 2, y), (y * 2 + 1, y * 2 + 4), (y + 8, y * 2 + 5))
     ]
+    places = [(weight_in.at[half_rows, pl.ds(c, 128)], weight.at[z_hi // 2, z_hi % 2, x, core, :, pl.ds(c, 128)]) for c in tiles]
+    weight_copies = [pltpu.make_async_copy(*place, local_sem.at[9 + i]) for i, place in enumerate(places)]
+    for made in weight_copies:
+        made.start()
     for made in own_copies:
         made.start()
-    peers = [partner, y_after, y_before, *x_peers, low_peer, *high_peers]
-    peers += [next_row, last_row, next_frame, last_frame]
+    others = [{"ta": ta, "ha": (ha + s) % 16} for s in range(1, 16)]
+    y_far = at_place(z_lo, (y + 2) % 4, core, z_hi, x)
+    peers = [partner, y_after, y_far, y_before, low_peer, next_frame, last_frame, *others]
     barrier = pltpu.get_barrier_semaphore()
     for peer in peers:
         pl.semaphore_signal(barrier, inc=1, device_id=peer, device_id_type=pl.DeviceIdType.MESH)
@@ -251,61 +274,96 @@
     start = copies.start
     mine = pl.ds(1, 4)
 
-    def quarter(p):
-        return pl.ds(pl.multiple_of(p * 256, 256), 256)
-
-    def pieces(cols):
-        piece = weight_in.at[half_rows, cols]
-        return [start(piece, weight.at[z_hi, x, core, :, cols], peer) for peer in high_peers]
+    def share(p, first, width):
+        return pl.ds(pl.multiple_of(first + p * width, 128), width)
 
     def over_x(p, begin, size):
-        return weight.at[pl.ds(begin, size), p, core, :, quarter(y)]
-
-    def over_x_direct(p, begin, size):
-        return weight.at[pl.ds(begin, size), p, core, :, direct]
-
-    def over_y(p, begin, size):
-        return weight.at[pl.ds(begin, size), :, core, :, quarter(p)]
+        zs = pl.ds(begin // 2, size // 2)
+        return (weight.at[zs, 0, p, core, :, share(y, 0, 256)], weight.at[zs, 1, p, core, :, share(y, 0, 128)])
+
+    def over_y_direct(p, begin, size):
+        zs = pl.ds(begin // 2, size // 2)
+        return (weight.at[zs, 0, x, core, :, share(p, 1024, 128)], weight.at[zs, 1, x, core, :, share(p, 512, 256)])
+
+    def over_y(group):
+        def blocks(p, begin, size):
+            xs = pl.ds(begin, size)
+            return (
+                weight.at[group, 0, xs, core, :, share(p, 0, 256)],
+                weight.at[group, 1, xs, core, :, share(p, 0, 128)],
+            )
+
+        return blocks
+
+    def over_x_direct(group):
+        def blocks(p, begin, size):
+            return (
+                weight.at[group, 0, p, core, :, pl.ds(1024 + begin * 128, size * 128)],
+                weight.at[group, 1, p, core, :, pl.ds(512 + begin * 256, size * 256)],
+            )
+
+        return blocks
 
     gather_x = RingGather(copies, over_x, x, x_after, x_before)
-    gather_d = RingGather(copies, over_x_direct, x, x_after, x_before)
-    gather_y = RingGather(copies, over_y, y, y_after, y_before)
-    shared_in = pieces(shared)
-    near, far = pl.ds(0, 896), pl.ds(896, 640)
+    gather_e = RingGather(copies, over_y_direct, y, y_after, y_before)
+    gather_y = [RingGather(copies, over_y(g), y, y_after, y_before) for g in range(2)]
+    gather_d = [RingGather(copies, over_x_direct(g), x, x_after, x_before) for g in range(2)]
+    swaps = [[], []]
+
+    def swap_parts(group, parts):
+        swaps[group].extend(start(part, part, partner) for part in parts)
+
+    def swap_y(group, *steps):
+        for step in steps:
+            swap_parts(group, gather_y[group].blocks((y + step) % 4, 0, 4))
+
+    def swap_d(group):
+        swap_parts(group, (weight.at[group, 0, :, core, :, pl.ds(1024, 512)], weight.at[group, 1, :, core, :, pl.ds(512, 1024)]))
+
+    pieces = [start(src, dst, peer) for src, dst in places for peer in high_peers]
+    near, far = pl.ds(0, NEAR), pl.ds(NEAR, FAR)
     rows_in = [
         RowSwap(
             copies,
             relay_sems.at[i],
             spot,
-            (kv_in.at[:, :, 3, :, cols], kv.at[:, mine, 0, :, cols]),
-            (kv_in.at[:, :, 0, :, cols], kv.at[:, mine, 5, :, cols]),
+            (kv_in.at[part, :, 3, :, cols], kv.at[part, mine, 0, :, cols]),
+            (kv_in.at[part, :, 0, :, cols], kv.at[part, mine, 5, :, cols]),
             relay,
         )
-        for i, (cols, relay) in enumerate(((far, relay_kv), (near, None)))
+        for i, (part, cols, relay) in enumerate(
+            ((0, far, relay_kv.at[0]), (1, far, relay_kv.at[1]), (pl.ds(0, 2), near, None))
+        )
     ]
     frames_in = [
         start(kv_in.at[:, 3], kv.at[:, 0, mine], next_frame),
         start(kv_in.at[:, 0], kv.at[:, 5, mine], last_frame),
     ]
     up_swap = start(up_hbm, up_in, partner)
-    for made in shared_in:
+    for made in weight_copies:
+        made.wait()
+    for made in pieces:
         made.wait_recv()
-    own_copies[3].wait()
     gather_x.start()
+    gather_e.start()
+    rows_in[0].forward()
+    rows_in[1].forward()
+    gather_e.middle()
     gather_x.middle()
-    rows_in[0].forward()
+    gather_e.end()
     for swap in rows_in:
         swap.wait()
-    for made in (*own_copies[:3], own_copies[4]):
+    for made in own_copies:
         made.wait()
     corners_in = []
     for frame, goal, device in ((4, 0, next_frame), (1, 5, last_frame)):
         for row in (0, 5):
             corners_in.append(start(kv.at[:, frame, row], kv.at[:, goal, row], device))
-    direct_in = pieces(direct)
+    gather_d[0].start()
     gather_x.end()
-    gather_y.start()
-    swaps = [start(over_y(y, 0, 4), over_y(y, 0, 4), partner)]
+    gather_y[0].start()
+    swap_y(0, 0)
+    swap_y(1, 0)
     for made in (*frames_in, *corners_in):
         made.wait_recv()
 
@@ -315,7 +373,6 @@
     turn = (group >> 2 & 1) * 8 + (group & 3) * 2 + (group >> 3)
     wanted = (out_row >> 1 & 3) * 32 + turn * 2 + (out_row & 1)
     order = (wanted == feature).astype(bf16)
-    eye = (out_row == feature).astype(bf16)
     scaling = HEAD_DIM ** (-0.5)
 
     def forward(pair, carry):
@@ -350,7 +407,7 @@
             grad_probs = lax.dot_general(values, grad, ACROSS, preferred_element_type=f32)
             delta = jnp.sum(probs * grad_probs, axis=0, keepdims=True)
             grad_scores = (probs * (grad_probs - delta) * scaling).astype(bf16)
-            keys_t = lax.dot_general(eye, keys, ACROSS, preferred_element_type=f32).astype(bf16)
+            keys_t = keys.T
             dq[:, cols] = jnp.dot(keys_t, grad_scores, preferred_element_type=f32).T.astype(bf16)
             grad_keys = jnp.dot(grad_scores, q[:, cols], preferred_element_type=f32).astype(bf16)
             grad_values = jnp.dot(probs.astype(bf16), grad, preferred_element_type=f32).astype(bf16)
@@ -358,19 +415,31 @@
             dkv[1, :, :, :, cols] = grad_values.reshape(6, 6, 16, 128)
         return carry
 
-    for made in direct_in:
+    at_swaps = []
+
+    def swap_outputs(half):
+        rows = pl.ds(half * 48, 48)
+        at_swaps.append(start(at.at[pl.ds((1 - core) * 8, 8), rows], at_in.at[:, rows], partner))
+
+    lax.fori_loop(0, 3, forward, 0)
+    swap_outputs(0)
+    gather_d[0].middle()
+    gather_d[1].start()
+    gather_y[0].middle()
+    gather_y[1].start()
+    swap_y(0, 3, 1)
+    lax.fori_loop(3, 6, forward, 0)
+    swap_outputs(1)
+    gather_d[0].end()
+    swap_d(0)
+    gather_y[0].end()
+    swap_y(0, 2)
+    gather_d[1].middle()
+    gather_y[1].middle()
+    swap_y(1, 3, 1)
+    up_swap.wait_recv()
+    for made in at_swaps:
         made.wait_recv()
-    gather_d.start()
-    lax.fori_loop(0, 3, forward, 0)
-    gather_y.middle()
-    for step in (3, 1):
-        part = over_y((y + step) % 4, 0, 4)
-        swaps.append(start(part, part, partner))
-    lax.fori_loop(3, 6, forward, 0)
-    at_swap = start(at.at[pl.ds((1 - core) * 8, 8)], at_in, partner)
-    gather_d.middle()
-    up_swap.wait_recv()
-    at_swap.wait_recv()
 
     def product(part, begin, width):
         a = at[pl.ds(core * 8 + part * 4, 4)].reshape(384, 256)
@@ -381,8 +450,9 @@
 
     ring_a = RingSum(copies, first_a, y, y_after, y_before, rings[0])
     ring_b = RingSum(copies, first_b, x, x_after, x_before, rings[1])
-    ring_c = RingSum(copies, second_a, x, x_after, x_before, rings[2])
-    ring_d = RingSum(copies, second_b, y, y_after, y_before, rings[3])
+    sum_a = DirectSum(copies, second_a, x, x_peers, came_a)
+    y_peers = [at_place(z_lo, (y + s) % 4, core, z_hi, x) for s in (1, 2, 3)]
+    sum_b = DirectSum(copies, second_b, y, y_peers, came_b)
     for goal in range(4):
         block = product(1, goal * 384, 384)
         for half in range(2):
@@ -393,35 +463,29 @@
         for goal in range(4):
             first_a[goal, half] = block[goal * 96 : goal * 96 + 96]
     ring_a.start()
-    gather_d.end()
-    part = weight.at[:, :, core, :, direct]
-    swaps.append(start(part, part, partner))
-    gather_y.end()
-    part = over_y((y + 2) % 4, 0, 4)
-    swaps.append(start(part, part, partner))
-    for made in swaps:
+    for made in swaps[0]:
         made.wait_recv()
     weight_rows = weight.reshape(1536, 1536)
     inner, outer = pl.ds(2, 2), pl.ds(1, 2)
 
-    def frames_out(half):
-        cols = pl.ds(half * 768, 768)
+    def frames_out(third):
+        cols = pl.ds(third * 512, 512)
         sides = (
             start(dkv.at[:, 5, :, :, cols], from_left.at[:, :, :, cols], next_frame),
             start(dkv.at[:, 0, :, :, cols], from_right.at[:, :, :, cols], last_frame),
         )
         rows = RowSwap(
             copies,
-            relay_sems.at[2 + half],
+            relay_sems.at[3 + third],
             spot,
             (dkv.at[:, inner, 5, :, cols], from_above.at[:, outer, :, cols]),
             (dkv.at[:, inner, 0, :, cols], from_below.at[:, outer, :, cols]),
-            relay_grad.at[half],
+            relay_grad.at[third],
         )
         return sides, rows
 
-    def rows_out(half, sides):
-        cols = pl.ds(half * 768, 768)
+    def rows_out(third, sides):
+        cols = pl.ds(third * 512, 512)
         made = []
         for side, frame, came, goal in ((sides[0], 1, from_left, 0), (sides[1], 4, from_right, 3)):
             side.wait_recv()
@@ -432,47 +496,47 @@
         return made
 
     lax.fori_loop(0, 2, backward, 0)
+    gather_d[1].end()
+    swap_d(1)
+    gather_y[1].end()
+    swap_y(1, 2)
+    sides_0, inner_0 = frames_out(0)
+    lax.fori_loop(2, 3, backward, 0)
+    for made in swaps[1]:
+        made.wait_recv()
+    lax.fori_loop(3, 4, backward, 0)
     ring_b.middle()
     ring_a.middle()
-    lax.fori_loop(2, 3, backward, 0)
-    sides_0, inner_0 = frames_out(0)
-    lax.fori_loop(3, 4, backward, 0)
+    sides_1, inner_1 = frames_out(1)
+    outer_out = rows_out(0, sides_0)
+    inner_0.forward()
+    lax.fori_loop(4, 5, backward, 0)
     for half in range(2):
         block = ring_b.end(half).astype(bf16)
         for goal in range(2):
-            for row in range(2):
-                begin = goal * 96 + row * 48
-                second_b[half * 2 + goal, row] = block[begin : begin + 48]
-    ring_d.start()
+            second_b[half * 2 + goal] = block[goal * 96 : goal * 96 + 96]
+    sum_b.start()
     for half in range(2):
         block = ring_a.end(half).astype(bf16)
         for goal in range(2):
-            for row in range(2):
-                second_a[half * 2 + goal, row] = block[row * 48 : row * 48 + 48, goal * 384 : goal * 384 + 384]
-    ring_c.start()
-    lax.fori_loop(4, 5, backward, 0)
-    outer_out = rows_out(0, sides_0)
-    ring_d.middle()
-    ring_c.middle()
+            second_a[half * 2 + goal] = block[:, goal * 384 : goal * 384 + 384]
+    sum_a.start()
     lax.fori_loop(5, 6, backward, 0)
-    sides_1, inner_1 = frames_out(1)
+    sides_2, inner_2 = frames_out(2)
     results = [pltpu.make_async_copy(dq, dq_out, local_sem.at[5])]
     results[0].start()
-    for part, ring in ((1, ring_d), (0, ring_c)):
-        for row in range(2):
-            pair_sums[part, row * 48 : row * 48 + 48] = ring.end(row).astype(bf16)
+    outer_out += rows_out(1, sides_1)
+    inner_1.forward()
+    pair_sums[1] = sum_b.end().astype(bf16)
+    pair_sums[0] = sum_a.end().astype(bf16)
     low = start(pair_sums.at[1 - z_lo], pair_in, low_peer)
-    inner_0.forward()
-    outer_out += rows_out(1, sides_1)
+    outer_out += rows_out(2, sides_2)
     low.wait_recv()
-    total = pair_sums[z_lo].astype(f32) + pair_in[...].astype(f32)
-    tall[...] = total.astype(bf16)
-    highs = []
-    for i in range(3):
-        chosen = pick[pl.ds(pl.multiple_of((z_hi + i + 1) % 4 * 48, 16), 48), :]
-        tall_out[i] = jnp.dot(chosen, tall[...], preferred_element_type=f32).astype(bf16)
-        highs.append(start(tall_out.at[i], tall_in.at[i], high_peers[i]))
-    inner_1.forward()
+    tall = (pair_sums[z_lo].astype(f32) + pair_in[...].astype(f32)).astype(bf16)
+    slots_out[...] = jnp.dot(pick[...], tall, preferred_element_type=f32).astype(bf16).reshape(16, 16, 384)
+    lasts = [start(slots_out.at[(ha + i + 1) % 16], slots_in.at[ha], others[i]) for i in range(15)]
+    slots_in[ha] = slots_out[ha]
+    inner_2.forward()
     for i in range(2):
         dkv_out[i, :, 1:3] = dkv[i, 1:5, 2:4]
         for f, came in ((0, from_left), (3, from_right)):
@@ -484,19 +548,8 @@
         results.append(made)
 
     result(6, pl.ds(1, 2))
-    chosen = pick[pl.ds(pl.multiple_of(z_hi * 48, 16), 48), :]
-    total = jnp.dot(chosen, tall[...], preferred_element_type=f32)
-    for i in range(3):
-        highs[i].wait_recv()
-        total += tall_in[i].astype(f32)
-    total = total * 0.00390625
-    for goal in range(4):
-        last_out[goal, 0:12] = total[goal * 12 : goal * 12 + 12]
-        last_out[goal, 12:16] = jnp.zeros((4, 384), f32)
-    lasts = [start(last_out.at[(x + i + 1) % 4], last_in.at[x], x_peers[i]) for i in range(3)]
-    last_in[x] = last_out[x]
-    inner_0.wait()
-    inner_1.wait()
+    for swap in (inner_0, inner_1, inner_2):
+        swap.wait()
     for made in outer_out:
         made.wait_recv()
     for i in range(2):
@@ -509,12 +562,13 @@
     for made in lasts:
         made.wait_recv()
     for goal in range(4):
+        total = sum(slots_in[i * 4 + goal].astype(f32) for i in range(4)) * 0.00390625
         for slot in range(6):
-            owned[slot, :, goal * 384 : goal * 384 + 384] = last_in[goal, slot * 2 : slot * 2 + 2]
+            owned[slot, :, goal * 384 : goal * 384 + 384] = total[slot * 2 : slot * 2 + 2]
     for made in results:
         made.wait()
     copies.drain()
-    for swap in (rows_in[0], inner_0, inner_1):
+    for swap in (*rows_in[:2], inner_0, inner_1, inner_2):
         swap.drain()
 
 
@@ -534,7 +588,7 @@
         scratch_shapes=[
             pltpu.VMEM((2, 6, 6, 16, 1536), bf16),
             pltpu.VMEM((2, 6, 6, 16, 1536), bf16),
-            pltpu.VMEM((4, 4, 2, 48, 1536), bf16),
+            pltpu.VMEM((2, 2, 4, 2, 48, 1536), bf16),
             pltpu.VMEM((12, 576, 256), jnp.float32),
             pltpu.VMEM((576, 256), jnp.int32),
             pltpu.VMEM((16, 96, 256), bf16),
@@ -546,31 +600,28 @@
             pltpu.VMEM((2, 4, 16, 1536), bf16),
             pltpu.VMEM((4, 2, 96, 768), bf16),
             pltpu.VMEM((4, 2, 192, 384), bf16),
-            pltpu.VMEM((4, 2, 48, 384), bf16),
-            pltpu.VMEM((4, 2, 48, 384), bf16),
+            pltpu.VMEM((4, 96, 384), bf16),
+            pltpu.VMEM((4, 96, 384), bf16),
+            pltpu.VMEM((3, 96, 384), bf16),
+            pltpu.VMEM((3, 96, 384), bf16),
             pltpu.VMEM((2, 96, 384), bf16),
             pltpu.VMEM((96, 384), bf16),
-            pltpu.VMEM((96, 384), bf16),
-            pltpu.VMEM((3, 48, 384), bf16),
-            pltpu.VMEM((3, 48, 384), bf16),
-            pltpu.VMEM((4, 16, 384), jnp.float32),
-            pltpu.VMEM((4, 16, 384), jnp.float32),
-            pltpu.VMEM((2, 4, 16, 640), bf16),
-            pltpu.VMEM((2, 2, 2, 16, 768), bf16),
+            pltpu.VMEM((16, 16, 384), bf16),
+            pltpu.VMEM((16, 16, 384), bf16),
+            pltpu.VMEM((2, 4, 16, FAR), bf16),
+            pltpu.VMEM((3, 2, 2, 16, 512), bf16),
             *ring_buffers(96, 768),
             *ring_buffers(192, 384),
-            *ring_buffers(48, 384),
-            *ring_buffers(48, 384),
             pltpu.VMEM((256, 1536), bf16),
             pltpu.VMEM((256, 1536), bf16),
             pltpu.VMEM((256, 1536), bf16),
             pltpu.VMEM((2, 4, 4, 16, 1536), bf16),
-            pltpu.VMEM((192, 96), bf16),
+            pltpu.VMEM((256, 96), bf16),
             pltpu.VMEM((HEADS, 256), jnp.int32),
-            pltpu.SemaphoreType.DMA((90,)),
-            pltpu.SemaphoreType.DMA((90,)),
-            pltpu.SemaphoreType.DMA((4, 3)),
-            pltpu.SemaphoreType.DMA((9,)),
+            pltpu.SemaphoreType.DMA((160,)),
+            pltpu.SemaphoreType.DMA((160,)),
+            pltpu.SemaphoreType.DMA((6, 3)),
+            pltpu.SemaphoreType.DMA((12,)),
         ],
         compiler_params=pltpu.CompilerParams(
             collective_id=1, has_side_effects=True, vmem_limit_bytes=56 * 1024 * 1024

time: 102 us -> 90.2 us (0.88); the launches traced: 99.9 us -> 90.1 us
  Pallas kernels: 95.3 us -> 85.5 us
    pallas_call x1, Pallas kernels: 95.3 us -> 85.5 us  [run_block(): pl.pallas_call(block_kernel, out_shape=[jax.ShapeDtypeStruct((256, 1536),...]
where the time goes in v3:
time: 90.2 us; the launch traced here: 90.1 us
  Pallas kernels  85.5 us (95%)
  local copies, waits for them, and re-layouts  3.96 us (4%)
    pallas_call x1, Pallas kernels, run_block(): pl.pallas_call(block_kernel, out_shape=[jax.ShapeDtypeStruct((256, 1536),...  85.5 us
    unnamed x7, local copies, waits for them, and re-layouts  3.96 us

profile of v3, /device:TPU:6, one launch (start us, length us, event | category | flops | bytes accessed | tf_op | source)
XLA Modules:
  0.0 90.1 jit_solution(2401375646695353200)
XLA Ops:
  0.6 85.5 %shard_map.85 = (bf16[256,1536]{1,0:T(8,128)(2,1)}, bf16[2,4,4,16,1536]{4,3,2,1,0:T(8,128)(2,1)}, f32[6,2,1536]{2,1,0:T(2,128)}) custom-call(bf16[256,1536]{1,0:T(8,128)(2,1)} %bitcast.5, bf16[2,4,4,16,1536]{4,3,2,1,0:T(8,128)(2,1)} %kv_in.1, bf16[256,1536]{1,0:T(8,128)(2,1)} %bitcast.6, bf16[96,1536]{1,0:T(8,128)(2,1)} %weight_in.1, s32[3,12]{1,0:T(4,128)} %bitcast.7, ...), custom_call_target="tpu_custom_call" | custom-call | tf_op jit(solution)/shard_map/pallas_call | solution.py:579
  86.1 0.0 copy-start
  86.1 2.2 %copy.12 = bf16[4,4,16,1536]{3,2,1,0:T(8,128)(2,1)} copy(bf16[4,4,16,1536]{3,2,1,0:T(8,128)(2,1)} %bitcast.4) | data formatting | bytes 1572864
  88.3 0.0 copy-done
  88.3 0.0 copy-start.1
  88.3 1.1 %copy.13 = bf16[2,4,4,16,1536]{4,3,2,1,0:T(8,128)(2,1)} copy(bf16[2,4,4,16,1536]{4,3,2,1,0:T(8,128)(2,1)S(1)} %copy-done) | data formatting | bytes 3145728
  89.4 0.0 copy-done.1
  89.4 0.6 copy.14
Async XLA Ops:
  86.1 2.2 %copy-start = (bf16[2,4,4,16,1536]{4,3,2,1,0:T(8,128)(2,1)S(1)}, bf16[2,4,4,16,1536]{4,3,2,1,0:T(8,128)(2,1)}, u32[]{:S(2)}) copy-start(bf16[2,4,4,16,1536]{4,3,2,1,0:T(8,128)(2,1)} %get-tuple-element.13) | copy-start | bytes 4718596
  88.3 1.1 %copy-start.1 = (f32[6,2,1536]{2,1,0:T(2,128)S(1)}, f32[6,2,1536]{2,1,0:T(2,128)}, u32[]{:S(2)}) copy-start(f32[6,2,1536]{2,1,0:T(2,128)} %get-tuple-element.14) | copy-start | bytes 221188

commit v4 on v3

--- a/solution.py
+++ b/solution.py
@@ -1,3 +1,5 @@
+import math
+
 import jax
 import jax.numpy as jnp
 from jax import lax
@@ -7,7 +9,8 @@
 
 HEADS = 12
 HEAD_DIM = 128
-NEAR, FAR = 896, 640
+PARTS = ((0, 512), (512, 768), (1280, 256))
+MEASURE = 45088
 ACROSS = (((1,), (1,)), ((), ()))
 
 
@@ -20,75 +23,91 @@
     return {"ta": z_lo * 8 + y * 2 + core, "ha": z_hi * 4 + x}
 
 
+def size_of(ref):
+    return math.prod(ref.shape) * (ref.dtype.itemsize // 2)
+
+
 class Copies:
-    def __init__(self, send, recv):
-        self.send, self.recv, self.made, self.count = send, recv, [], 0
-
-    def make(self, src, dst, device, send=None, recv=None):
-        self.count += recv is None
-        return pltpu.make_async_remote_copy(
-            src_ref=src,
-            dst_ref=dst,
-            send_sem=self.send.at[self.count - 1] if send is None else send,
-            recv_sem=self.recv.at[self.count - 1] if recv is None else recv,
-            device_id=device,
-            device_id_type=pl.DeviceIdType.MESH,
+    def __init__(self, send, recv, measure):
+        self.send, self.recv, self.measure, self.sent, self.count = send, recv, measure, 0, 0
+
+    def group(self):
+        made = Group(self, self.recv.at[self.count])
+        self.count += 1
+        return made
+
+    def wait(self, sem, size):
+        ref = self.measure.at[pl.ds(0, size // 128)]
+        pltpu.make_async_copy(ref, ref, sem).wait()
+
+    def drain(self):
+        self.wait(self.send, self.sent)
+
+
+def remote(src, dst, send, recv, device):
+    return pltpu.make_async_remote_copy(
+        src_ref=src,
+        dst_ref=dst,
+        send_sem=send,
+        recv_sem=recv,
+        device_id=device,
+        device_id_type=pl.DeviceIdType.MESH,
+    )
+
+
+class Group:
+    def __init__(self, copies, sem):
+        self.copies, self.sem, self.size = copies, sem, 0
+
+    def start(self, src, dst, device):
+        self.size += size_of(src)
+        self.copies.sent += size_of(src)
+        remote(src, dst, self.copies.send, self.sem, device).start()
+
+    def wait(self):
+        self.copies.wait(self.sem, self.size)
+
+
+class RowSwap:
+    def __init__(self, copies, groups, relay_sems, spot, up, down, relay):
+        self.x, next_row, last_row, x_after, x_before, high_after, high_before = spot
+        up_group, down_group = groups
+        if relay is None:
+            up_group.start(*up, next_row)
+            down_group.start(*down, last_row)
+            return
+        first, back, onward = (relay_sems.at[i] for i in range(3))
+        up_group.size += size_of(up[0])
+        down_group.size += size_of(down[0])
+        direct = (
+            remote(*up, first, up_group.sem, next_row),
+            remote(*down, first, down_group.sem, last_row),
         )
-
-    def start(self, src, dst, device):
-        made = self.make(src, dst, device)
-        made.start()
-        self.made.append(made)
-        return made
-
-    def drain(self):
-        for made in self.made:
-            made.wait_send()
-
-
-class RowSwap:
-    def __init__(self, copies, relay_sems, spot, up, down, relay):
-        self.x, next_row, last_row, x_after, x_before, high_after, high_before = spot
-        self.relayed = relay is not None
-        if not self.relayed:
-            self.up, self.down = copies.start(*up, next_row), copies.start(*down, last_row)
-            return
-        self.up, self.down = copies.make(*up, next_row), copies.make(*down, last_row)
-        out, back, onward = (relay_sems.at[i] for i in range(3))
-        recv = copies.count - 2
-        self.up_relay = copies.make(up[0], relay, x_after, out, back)
-        self.down_relay = copies.make(down[0], relay, x_before, out, back)
-        self.up_forward = copies.make(relay, up[1], high_after, onward, copies.recv.at[recv])
-        self.down_forward = copies.make(relay, down[1], high_before, onward, copies.recv.at[recv + 1])
-        for edge, direct, relayed in ((3, self.up, self.up_relay), (0, self.down, self.down_relay)):
+        self.relayed = (
+            remote(up[0], relay, first, back, x_after),
+            remote(down[0], relay, first, back, x_before),
+        )
+        self.onward = (
+            remote(relay, up[1], onward, up_group.sem, high_after),
+            remote(relay, down[1], onward, down_group.sem, high_before),
+        )
+        self.done = lambda: copies.wait(first, size_of(up[0]) + size_of(down[0]))
+        for edge, straight, relayed in zip((3, 0), direct, self.relayed):
             pl.when(self.x == edge)(relayed.start)
-            pl.when(self.x != edge)(direct.start)
+            pl.when(self.x != edge)(straight.start)
 
     def forward(self):
-        for edge, relayed, onward in (
-            (0, self.up_relay, self.up_forward),
-            (3, self.down_relay, self.down_forward),
-        ):
+        for edge, relayed, onward in zip((0, 3), self.relayed, self.onward):
 
             @pl.when(self.x == edge)
             def _():
                 relayed.wait_recv()
                 onward.start()
 
-    def wait(self):
-        self.up.wait_recv()
-        self.down.wait_recv()
-
     def drain(self):
-        pl.when(self.x != 3)(self.up.wait_send)
-        pl.when(self.x != 0)(self.down.wait_send)
-        for edge, made in (
-            (3, self.up_relay),
-            (0, self.down_relay),
-            (0, self.up_forward),
-            (3, self.down_forward),
-        ):
-            pl.when(self.x == edge)(made.wait_send)
+        self.done()
+        for edge, onward in zip((0, 3), self.onward):
+            pl.when(self.x == edge)(onward.wait_send)
 
 
 class RingSum:
@@ -97,38 +116,36 @@
         self.left, self.right, self.via_left, self.via_right, self.stage = bufs
 
     def start(self):
-        pos, src, start = self.pos, self.src, self.copies.start
+        pos, src = self.pos, self.src
         far = (pos + 2) % 4
-        self.first = [
-            start(src.at[far, 0], self.via_left, self.after),
-            start(src.at[far, 1], self.via_right, self.before),
-        ]
-        self.left_1 = start(src.at[(pos + 1) % 4, 1], self.left.at[1], self.after)
-        self.right_0 = start(src.at[(pos + 3) % 4, 0], self.right.at[0], self.before)
+        self.first = [self.copies.group(), self.copies.group()]
+        self.rest = self.copies.group()
+        self.first[0].start(src.at[far, 0], self.via_left, self.after)
+        self.first[1].start(src.at[far, 1], self.via_right, self.before)
+        self.rest.start(src.at[(pos + 1) % 4, 1], self.left.at[1], self.after)
+        self.rest.start(src.at[(pos + 3) % 4, 0], self.right.at[0], self.before)
 
     def middle(self):
         pos, src = self.pos, self.src
-        made = []
         for index, (via, goal, dst, device) in enumerate(
             (
                 (self.via_left, (pos + 1) % 4, self.left, self.after),
                 (self.via_right, (pos + 3) % 4, self.right, self.before),
             )
         ):
-            self.first[index].wait_recv()
+            self.first[index].wait()
             total = via[...].astype(jnp.float32) + src[goal, index].astype(jnp.float32)
             self.stage[index] = total.astype(self.stage.dtype)
-            made.append(self.copies.start(self.stage.at[index], dst.at[index], device))
-        self.left_0, self.right_1 = made
-
-    def end(self, half):
-        for made in ((self.right_0, self.left_0), (self.left_1, self.right_1))[half]:
-            made.wait_recv()
-        return (
+            self.rest.start(self.stage.at[index], dst.at[index], device)
+
+    def end(self):
+        self.rest.wait()
+        return [
             self.src[self.pos, half].astype(jnp.float32)
             + self.left[half].astype(jnp.float32)
             + self.right[half].astype(jnp.float32)
-        )
+            for half in range(2)
+        ]
 
 
 class DirectSum:
@@ -136,17 +153,13 @@
         self.copies, self.src, self.pos, self.peers, self.came = copies, src, pos, peers, came
 
     def start(self):
-        self.made = [
-            self.copies.start(self.src.at[(self.pos + i + 1) % 4], self.came.at[i], self.peers[i])
-            for i in range(3)
-        ]
+        self.group = self.copies.group()
+        for i in range(3):
+            self.group.start(self.src.at[(self.pos + i + 1) % 4], self.came.at[i], self.peers[i])
 
     def end(self):
-        total = self.src[self.pos].astype(jnp.float32)
-        for i in range(3):
-            self.made[i].wait_recv()
-            total += self.came[i].astype(jnp.float32)
-        return total
+        self.group.wait()
+        return sum((self.came[i].astype(jnp.float32) for i in range(3)), self.src[self.pos].astype(jnp.float32))
 
 
 def ring_buffers(rows, columns):
@@ -163,25 +176,23 @@
     def __init__(self, copies, blocks, pos, after, before):
         self.copies, self.blocks, self.pos, self.after, self.before = copies, blocks, pos, after, before
 
-    def send(self, step, begin, size, device):
-        parts = self.blocks((self.pos + step) % 4, begin, size)
-        return [self.copies.start(part, part, device) for part in parts]
+    def send(self, group, step, begin, size, device):
+        for part in self.blocks((self.pos + step) % 4, begin, size):
+            group.start(part, part, device)
 
     def start(self):
-        self.from_before = self.send(0, 0, 4, self.after)
-        self.from_after = self.send(0, 0, 4, self.before)
+        self.from_before, self.from_after, self.far = (self.copies.group() for _ in range(3))
+        self.send(self.from_before, 0, 0, 4, self.after)
+        self.send(self.from_after, 0, 0, 4, self.before)
 
     def middle(self):
-        for made in self.from_before:
-            made.wait_recv()
-        self.far = self.send(3, 0, 2, self.after)
-        for made in self.from_after:
-            made.wait_recv()
-        self.far += self.send(1, 2, 2, self.before)
+        self.from_before.wait()
+        self.send(self.far, 3, 0, 2, self.after)
+        self.from_after.wait()
+        self.send(self.far, 1, 2, 2, self.before)
 
     def end(self):
-        for made in self.far:
-            made.wait_recv()
+        self.far.wait()
 
 
 def window_bits(need):
@@ -231,7 +242,7 @@
     slots_out, slots_in, relay_kv, relay_grad = refs[20:24]
     rings = [refs[24 + 5 * i : 29 + 5 * i] for i in range(2)]
     q, up, dq, dkv_out, pick, blocks = refs[34:40]
-    send, recv, relay_sems, local_sem = refs[40:]
+    measure, send, recv, relay_sems, local_sem = refs[40:]
     z_lo, y, core, z_hi, x = place()
     ta, ha = lax.axis_index("ta"), lax.axis_index("ha")
     partner = at_place(z_lo, y, 1 - core, z_hi, x)
@@ -270,8 +281,13 @@
     slot_picks(bucket_owner, pick)
     pl.semaphore_wait(barrier, len(peers))
 
-    copies = Copies(send, recv)
-    start = copies.start
+    copies = Copies(send, recv, measure)
+
+    def start(src, dst, device):
+        group = copies.group()
+        group.start(src, dst, device)
+        return group
+
     mine = pl.ds(1, 4)
 
     def share(p, first, width):
@@ -285,87 +301,75 @@
         zs = pl.ds(begin // 2, size // 2)
         return (weight.at[zs, 0, x, core, :, share(p, 1024, 128)], weight.at[zs, 1, x, core, :, share(p, 512, 256)])
 
-    def over_y(group):
-        def blocks(p, begin, size):
-            xs = pl.ds(begin, size)
-            return (
-                weight.at[group, 0, xs, core, :, share(p, 0, 256)],
-                weight.at[group, 1, xs, core, :, share(p, 0, 128)],
-            )
-
-        return blocks
-
-    def over_x_direct(group):
-        def blocks(p, begin, size):
-            return (
-                weight.at[group, 0, p, core, :, pl.ds(1024 + begin * 128, size * 128)],
-                weight.at[group, 1, p, core, :, pl.ds(512 + begin * 256, size * 256)],
-            )
-
-        return blocks
+    def over_y(p, begin, size):
+        xs = pl.ds(begin, size)
+        return (weight.at[:, 0, xs, core, :, share(p, 0, 256)], weight.at[:, 1, xs, core, :, share(p, 0, 128)])
+
+    def over_x_direct(p, begin, size):
+        return (
+            weight.at[:, 0, p, core, :, pl.ds(1024 + begin * 128, size * 128)],
+            weight.at[:, 1, p, core, :, pl.ds(512 + begin * 256, size * 256)],
+        )
 
     gather_x = RingGather(copies, over_x, x, x_after, x_before)
     gather_e = RingGather(copies, over_y_direct, y, y_after, y_before)
-    gather_y = [RingGather(copies, over_y(g), y, y_after, y_before) for g in range(2)]
-    gather_d = [RingGather(copies, over_x_direct(g), x, x_after, x_before) for g in range(2)]
-    swaps = [[], []]
-
-    def swap_parts(group, parts):
-        swaps[group].extend(start(part, part, partner) for part in parts)
-
-    def swap_y(group, *steps):
+    gather_y = RingGather(copies, over_y, y, y_after, y_before)
+    gather_d = RingGather(copies, over_x_direct, x, x_after, x_before)
+    swaps = copies.group()
+
+    def swap_parts(*steps):
         for step in steps:
-            swap_parts(group, gather_y[group].blocks((y + step) % 4, 0, 4))
-
-    def swap_d(group):
-        swap_parts(group, (weight.at[group, 0, :, core, :, pl.ds(1024, 512)], weight.at[group, 1, :, core, :, pl.ds(512, 1024)]))
-
-    pieces = [start(src, dst, peer) for src, dst in places for peer in high_peers]
-    near, far = pl.ds(0, NEAR), pl.ds(NEAR, FAR)
+            gather_d.send(swaps, step, 0, 4, partner)
+            gather_y.send(swaps, step, 0, 4, partner)
+
+    pieces = copies.group()
+    for src, dst in places:
+        for peer in high_peers:
+            pieces.start(src, dst, peer)
+    edge_groups, rows_groups = ((copies.group(), copies.group()) for _ in range(2))
+    for frame in (3, 0):
+        edge_groups[0].start(kv_in.at[:, frame, 3], kv.at[:, frame + 1, 0], next_row)
+        edge_groups[1].start(kv_in.at[:, frame, 0], kv.at[:, frame + 1, 5], last_row)
     rows_in = [
         RowSwap(
             copies,
+            rows_groups,
             relay_sems.at[i],
             spot,
-            (kv_in.at[part, :, 3, :, cols], kv.at[part, mine, 0, :, cols]),
-            (kv_in.at[part, :, 0, :, cols], kv.at[part, mine, 5, :, cols]),
-            relay,
+            (kv_in.at[i, pl.ds(1, 2), 3], kv.at[i, pl.ds(2, 2), 0]),
+            (kv_in.at[i, pl.ds(1, 2), 0], kv.at[i, pl.ds(2, 2), 5]),
+            relay_kv.at[i],
         )
-        for i, (part, cols, relay) in enumerate(
-            ((0, far, relay_kv.at[0]), (1, far, relay_kv.at[1]), (pl.ds(0, 2), near, None))
-        )
+        for i in range(2)
     ]
-    frames_in = [
-        start(kv_in.at[:, 3], kv.at[:, 0, mine], next_frame),
-        start(kv_in.at[:, 0], kv.at[:, 5, mine], last_frame),
-    ]
+    frames_in = copies.group()
+    frames_in.start(kv_in.at[:, 3], kv.at[:, 0, mine], next_frame)
+    frames_in.start(kv_in.at[:, 0], kv.at[:, 5, mine], last_frame)
     up_swap = start(up_hbm, up_in, partner)
     for made in weight_copies:
         made.wait()
-    for made in pieces:
-        made.wait_recv()
+    pieces.wait()
     gather_x.start()
     gather_e.start()
     rows_in[0].forward()
     rows_in[1].forward()
     gather_e.middle()
     gather_x.middle()
+    for group in edge_groups:
+        group.wait()
+    for frame, goal, device in ((4, 0, next_frame), (1, 5, last_frame)):
+        for row in (0, 5):
+            frames_in.start(kv.at[:, frame, row], kv.at[:, goal, row], device)
     gather_e.end()
-    for swap in rows_in:
-        swap.wait()
+    for group in rows_groups:
+        group.wait()
     for made in own_copies:
         made.wait()
-    corners_in = []
-    for frame, goal, device in ((4, 0, next_frame), (1, 5, last_frame)):
-        for row in (0, 5):
-            corners_in.append(start(kv.at[:, frame, row], kv.at[:, goal, row], device))
-    gather_d[0].start()
     gather_x.end()
-    gather_y[0].start()
-    swap_y(0, 0)
-    swap_y(1, 0)
-    for made in (*frames_in, *corners_in):
-        made.wait_recv()
+    gather_y.start()
+    gather_d.start()
+    swap_parts(0)
+    frames_in.wait()
 
     out_row = lax.broadcasted_iota(jnp.int32, (128, 128), 0)
     feature = lax.broadcasted_iota(jnp.int32, (128, 128), 1)
@@ -415,31 +419,21 @@
             dkv[1, :, :, :, cols] = grad_values.reshape(6, 6, 16, 128)
         return carry
 
-    at_swaps = []
+    at_swaps = copies.group()
 
     def swap_outputs(half):
         rows = pl.ds(half * 48, 48)
-        at_swaps.append(start(at.at[pl.ds((1 - core) * 8, 8), rows], at_in.at[:, rows], partner))
+        at_swaps.start(at.at[pl.ds((1 - core) * 8, 8), rows], at_in.at[:, rows], partner)
 
     lax.fori_loop(0, 3, forward, 0)
     swap_outputs(0)
-    gather_d[0].middle()
-    gather_d[1].start()
-    gather_y[0].middle()
-    gather_y[1].start()
-    swap_y(0, 3, 1)
     lax.fori_loop(3, 6, forward, 0)
     swap_outputs(1)
-    gather_d[0].end()
-    swap_d(0)
-    gather_y[0].end()
-    swap_y(0, 2)
-    gather_d[1].middle()
-    gather_y[1].middle()
-    swap_y(1, 3, 1)
-    up_swap.wait_recv()
-    for made in at_swaps:
-        made.wait_recv()
+    gather_d.middle()
+    gather_y.middle()
+    swap_parts(3, 1)
+    up_swap.wait()
+    at_swaps.wait()
 
     def product(part, begin, width):
         a = at[pl.ds(core * 8 + part * 4, 4)].reshape(384, 256)
@@ -463,78 +457,73 @@
         for goal in range(4):
             first_a[goal, half] = block[goal * 96 : goal * 96 + 96]
     ring_a.start()
-    for made in swaps[0]:
-        made.wait_recv()
+    gather_d.end()
+    gather_y.end()
+    swap_parts(2)
+    swaps.wait()
     weight_rows = weight.reshape(1536, 1536)
     inner, outer = pl.ds(2, 2), pl.ds(1, 2)
+    rows_back = copies.group(), copies.group()
 
     def frames_out(third):
-        cols = pl.ds(third * 512, 512)
+        cols = pl.ds(*PARTS[third])
         sides = (
             start(dkv.at[:, 5, :, :, cols], from_left.at[:, :, :, cols], next_frame),
             start(dkv.at[:, 0, :, :, cols], from_right.at[:, :, :, cols], last_frame),
         )
         rows = RowSwap(
             copies,
-            relay_sems.at[3 + third],
+            rows_back,
+            relay_sems.at[2 + third],
             spot,
             (dkv.at[:, inner, 5, :, cols], from_above.at[:, outer, :, cols]),
             (dkv.at[:, inner, 0, :, cols], from_below.at[:, outer, :, cols]),
-            relay_grad.at[third],
+            relay_grad.at[third, :, :, :, pl.ds(0, PARTS[third][1])],
         )
         return sides, rows
 
     def rows_out(third, sides):
-        cols = pl.ds(third * 512, 512)
-        made = []
+        cols = pl.ds(*PARTS[third])
         for side, frame, came, goal in ((sides[0], 1, from_left, 0), (sides[1], 4, from_right, 3)):
-            side.wait_recv()
+            side.wait()
             total = dkv[:, frame, :, :, cols].astype(f32) + came[:, :, :, cols].astype(f32)
             came[:, :, :, cols] = total.astype(bf16)
-            made.append(start(came.at[:, 5, :, cols], from_above.at[:, goal, :, cols], next_row))
-            made.append(start(came.at[:, 0, :, cols], from_below.at[:, goal, :, cols], last_row))
-        return made
+            rows_back[0].start(came.at[:, 5, :, cols], from_above.at[:, goal, :, cols], next_row)
+            rows_back[1].start(came.at[:, 0, :, cols], from_below.at[:, goal, :, cols], last_row)
 
     lax.fori_loop(0, 2, backward, 0)
-    gather_d[1].end()
-    swap_d(1)
-    gather_y[1].end()
-    swap_y(1, 2)
     sides_0, inner_0 = frames_out(0)
     lax.fori_loop(2, 3, backward, 0)
-    for made in swaps[1]:
-        made.wait_recv()
-    lax.fori_loop(3, 4, backward, 0)
     ring_b.middle()
     ring_a.middle()
+    lax.fori_loop(3, 5, backward, 0)
     sides_1, inner_1 = frames_out(1)
-    outer_out = rows_out(0, sides_0)
+    rows_out(0, sides_0)
     inner_0.forward()
-    lax.fori_loop(4, 5, backward, 0)
-    for half in range(2):
-        block = ring_b.end(half).astype(bf16)
-        for goal in range(2):
-            second_b[half * 2 + goal] = block[goal * 96 : goal * 96 + 96]
-    sum_b.start()
-    for half in range(2):
-        block = ring_a.end(half).astype(bf16)
-        for goal in range(2):
-            second_a[half * 2 + goal] = block[:, goal * 384 : goal * 384 + 384]
-    sum_a.start()
     lax.fori_loop(5, 6, backward, 0)
     sides_2, inner_2 = frames_out(2)
     results = [pltpu.make_async_copy(dq, dq_out, local_sem.at[5])]
     results[0].start()
-    outer_out += rows_out(1, sides_1)
+    for half, block in enumerate(ring_b.end()):
+        for goal in range(2):
+            second_b[half * 2 + goal] = block[goal * 96 : goal * 96 + 96].astype(bf16)
+    sum_b.start()
+    for half, block in enumerate(ring_a.end()):
+        for goal in range(2):
+            second_a[half * 2 + goal] = block[:, goal * 384 : goal * 384 + 384].astype(bf16)
+    sum_a.start()
+    rows_out(1, sides_1)
     inner_1.forward()
     pair_sums[1] = sum_b.end().astype(bf16)
     pair_sums[0] = sum_a.end().astype(bf16)
     low = start(pair_sums.at[1 - z_lo], pair_in, low_peer)
-    outer_out += rows_out(2, sides_2)
-    low.wait_recv()
+    rows_out(2, sides_2)
+    low.wait()
     tall = (pair_sums[z_lo].astype(f32) + pair_in[...].astype(f32)).astype(bf16)
     slots_out[...] = jnp.dot(pick[...], tall, preferred_element_type=f32).astype(bf16).reshape(16, 16, 384)
-    lasts = [start(slots_out.at[(ha + i + 1) % 16], slots_in.at[ha], others[i]) for i in range(15)]
+    lasts = copies.group()
+    for i in range(15):
+        lasts.start(slots_out.at[(ha + i + 1) % 16], slots_in.at[ha], others[i])
     slots_in[ha] = slots_out[ha]
     inner_2.forward()
     for i in range(2):
@@ -548,10 +537,8 @@
         results.append(made)
 
     result(6, pl.ds(1, 2))
-    for swap in (inner_0, inner_1, inner_2):
-        swap.wait()
-    for made in outer_out:
-        made.wait_recv()
+    for group in rows_back:
+        group.wait()
     for i in range(2):
         for f, own in ((0, from_left), (1, None), (2, None), (3, from_right)):
             for r, came in ((0, from_above), (3, from_below)):
@@ -559,8 +546,7 @@
                 dkv_out[i, f, r] = (base.astype(f32) + came[i, f].astype(f32)).astype(bf16)
     result(7, pl.ds(0, 1))
     result(8, pl.ds(3, 1))
-    for made in lasts:
-        made.wait_recv()
+    lasts.wait()
     for goal in range(4):
         total = sum(slots_in[i * 4 + goal].astype(f32) for i in range(4)) * 0.00390625
         for slot in range(6):
@@ -568,7 +554,7 @@
     for made in results:
         made.wait()
     copies.drain()
-    for swap in (*rows_in[:2], inner_0, inner_1, inner_2):
+    for swap in (*rows_in, inner_0, inner_1, inner_2):
         swap.drain()
 
 
@@ -608,8 +594,8 @@
             pltpu.VMEM((96, 384), bf16),
             pltpu.VMEM((16, 16, 384), bf16),
             pltpu.VMEM((16, 16, 384), bf16),
-            pltpu.VMEM((2, 4, 16, FAR), bf16),
-            pltpu.VMEM((3, 2, 2, 16, 512), bf16),
+            pltpu.VMEM((2, 2, 16, 1536), bf16),
+            pltpu.VMEM((3, 2, 2, 16, 768), bf16),
             *ring_buffers(96, 768),
             *ring_buffers(192, 384),
             pltpu.VMEM((256, 1536), bf16),
@@ -618,9 +604,10 @@
             pltpu.VMEM((2, 4, 4, 16, 1536), bf16),
             pltpu.VMEM((256, 96), bf16),
             pltpu.VMEM((HEADS, 256), jnp.int32),
-            pltpu.SemaphoreType.DMA((160,)),
-            pltpu.SemaphoreType.DMA((160,)),
-            pltpu.SemaphoreType.DMA((6, 3)),
+            pltpu.VMEM((MEASURE, 128), bf16),
+            pltpu.SemaphoreType.DMA,
+            pltpu.SemaphoreType.DMA((50,)),
+            pltpu.SemaphoreType.DMA((5, 3)),
             pltpu.SemaphoreType.DMA((12,)),
         ],
         compiler_params=pltpu.CompilerParams(

time: 90.2 us -> 85.8 us (0.951)
  the two profiles are of different devices: /device:TPU:6 before, /device:TPU:1 now
where the time goes in v4:
time: 85.8 us; the launch traced here: 85.6 us
  Pallas kernels  81 us (94%)
  local copies, waits for them, and re-layouts  3.96 us (5%)
    pallas_call x1, Pallas kernels, run_block(): pl.pallas_call(block_kernel, out_shape=[jax.ShapeDtypeStruct((256, 1536),...  81 us
    unnamed x7, local copies, waits for them, and re-layouts  3.96 us

profile of v4, /device:TPU:1, one launch (start us, length us, event | category | flops | bytes accessed | tf_op | source)
XLA Modules:
  0.0 85.6 jit_solution(12946222938637431642)
XLA Ops:
  0.6 81.0 %shard_map.85 = (bf16[256,1536]{1,0:T(8,128)(2,1)}, bf16[2,4,4,16,1536]{4,3,2,1,0:T(8,128)(2,1)}, f32[6,2,1536]{2,1,0:T(2,128)}) custom-call(bf16[256,1536]{1,0:T(8,128)(2,1)} %bitcast.5, bf16[2,4,4,16,1536]{4,3,2,1,0:T(8,128)(2,1)} %kv_in.1, bf16[256,1536]{1,0:T(8,128)(2,1)} %bitcast.6, bf16[96,1536]{1,0:T(8,128)(2,1)} %weight_in.1, s32[3,12]{1,0:T(4,128)} %bitcast.7, ...), custom_call_target="tpu_custom_call" | custom-call | tf_op jit(solution)/shard_map/pallas_call | solution.py:565
  81.7 0.0 copy-start
  81.7 2.2 %copy.12 = bf16[4,4,16,1536]{3,2,1,0:T(8,128)(2,1)} copy(bf16[4,4,16,1536]{3,2,1,0:T(8,128)(2,1)} %bitcast.4) | data formatting | bytes 1572864
  83.9 0.0 copy-done
  83.9 0.0 copy-start.1
  83.9 1.1 %copy.13 = bf16[2,4,4,16,1536]{4,3,2,1,0:T(8,128)(2,1)} copy(bf16[2,4,4,16,1536]{4,3,2,1,0:T(8,128)(2,1)S(1)} %copy-done) | data formatting | bytes 3145728
  85.0 0.0 copy-done.1
  85.0 0.6 copy.14
Async XLA Ops:
  81.7 2.2 %copy-start = (bf16[2,4,4,16,1536]{4,3,2,1,0:T(8,128)(2,1)S(1)}, bf16[2,4,4,16,1536]{4,3,2,1,0:T(8,128)(2,1)}, u32[]{:S(2)}) copy-start(bf16[2,4,4,16,1536]{4,3,2,1,0:T(8,128)(2,1)} %get-tuple-element.13) | copy-start | bytes 4718596
  83.9 1.1 %copy-start.1 = (f32[6,2,1536]{2,1,0:T(2,128)S(1)}, f32[6,2,1536]{2,1,0:T(2,128)}, u32[]{:S(2)}) copy-start(f32[6,2,1536]{2,1,0:T(2,128)} %get-tuple-element.14) | copy-start | bytes 221188

commit v5 on v4

--- a/solution.py
+++ b/solution.py
@@ -346,6 +346,12 @@
     frames_in.start(kv_in.at[:, 3], kv.at[:, 0, mine], next_frame)
     frames_in.start(kv_in.at[:, 0], kv.at[:, 5, mine], last_frame)
     up_swap = start(up_hbm, up_in, partner)
+    def clear(head, carry):
+        probs_all[head, pl.ds(384, 192), pl.ds(0, 128)] = jnp.zeros((192, 128), f32)
+        probs_all[head, pl.ds(0, 192), pl.ds(128, 128)] = jnp.zeros((192, 128), f32)
+        return carry
+
+    lax.fori_loop(0, HEADS, clear, 0)
     for made in weight_copies:
         made.wait()
     pieces.wait()
@@ -361,14 +367,14 @@
         for row in (0, 5):
             frames_in.start(kv.at[:, frame, row], kv.at[:, goal, row], device)
     gather_e.end()
+    gather_x.end()
+    gather_y.start()
+    gather_d.start()
+    swap_parts(0)
     for group in rows_groups:
         group.wait()
     for made in own_copies:
         made.wait()
-    gather_x.end()
-    gather_y.start()
-    gather_d.start()
-    swap_parts(0)
     frames_in.wait()
 
     out_row = lax.broadcasted_iota(jnp.int32, (128, 128), 0)
@@ -386,14 +392,17 @@
             cols = pl.ds(pl.multiple_of(head * 128, 128), 128)
             keys, values = (kv[i, :, :, :, cols].reshape(576, 128) for i in range(2))
             block = blocks[pl.ds(head, 1), :]
-            scores = lax.dot_general(keys, q[:, cols], ACROSS, preferred_element_type=f32)
-            scores = jnp.where((need[...] & block) == 0, scores, -1e30)
-            highest = jnp.max(scores, axis=0, keepdims=True)
-            weights = jnp.exp2((scores - highest) * (scaling * 1.4426950408889634))
-            probs = weights * (1.0 / jnp.sum(weights, axis=0, keepdims=True))
-            probs_all[head] = probs
+            for half in range(2):
+                rows, tokens = pl.ds(half * 192, 384), pl.ds(half * 128, 128)
+                scores = lax.dot_general(
+                    keys[half * 192 : half * 192 + 384], q[tokens, cols], ACROSS, preferred_element_type=f32
+                )
+                scores = jnp.where((need[rows, tokens] & block[:, :128]) == 0, scores, -1e30)
+                highest = jnp.max(scores, axis=0, keepdims=True)
+                weights = jnp.exp2((scores - highest) * (scaling * 1.4426950408889634))
+                probs_all[head, rows, tokens] = weights * (1.0 / jnp.sum(weights, axis=0, keepdims=True))
             values_t = lax.dot_general(order, values, ACROSS, preferred_element_type=f32).astype(bf16)
-            out = jnp.dot(values_t, probs.astype(bf16), preferred_element_type=f32)
+            out = jnp.dot(values_t, probs_all[head].astype(bf16), preferred_element_type=f32)
             outs.append(out.reshape(16, 8, 256))
         at[:, pl.ds(pl.multiple_of(pair * 16, 16), 16), :] = jnp.concatenate(outs, axis=1).astype(bf16)
         return carry
@@ -606,7 +615,7 @@
             pltpu.VMEM((HEADS, 256), jnp.int32),
             pltpu.VMEM((MEASURE, 128), bf16),
             pltpu.SemaphoreType.DMA,
-            pltpu.SemaphoreType.DMA((50,)),
+            pltpu.SemaphoreType.DMA((40,)),
             pltpu.SemaphoreType.DMA((5, 3)),
             pltpu.SemaphoreType.DMA((12,)),
         ],

time: 85.8 us -> 84 us (0.979)
  the two profiles are of different devices: /device:TPU:1 before, /device:TPU:6 now
where the time goes in v5:
time: 84 us; the launch traced here: 83.9 us
  Pallas kernels  79.3 us (94%)
  local copies, waits for them, and re-layouts  3.96 us (5%)
    pallas_call x1, Pallas kernels, run_block(): pl.pallas_call(block_kernel, out_shape=[jax.ShapeDtypeStruct((256, 1536),...  79.3 us
    unnamed x7, local copies, waits for them, and re-layouts  3.96 us

profile of v5, /device:TPU:6, one launch (start us, length us, event | category | flops | bytes accessed | tf_op | source)
XLA Modules:
  0.0 83.9 jit_solution(3701047987792590515)
XLA Ops:
  0.6 79.3 %shard_map.85 = (bf16[256,1536]{1,0:T(8,128)(2,1)}, bf16[2,4,4,16,1536]{4,3,2,1,0:T(8,128)(2,1)}, f32[6,2,1536]{2,1,0:T(2,128)}) custom-call(bf16[256,1536]{1,0:T(8,128)(2,1)} %bitcast.5, bf16[2,4,4,16,1536]{4,3,2,1,0:T(8,128)(2,1)} %kv_in.1, bf16[256,1536]{1,0:T(8,128)(2,1)} %bitcast.6, bf16[96,1536]{1,0:T(8,128)(2,1)} %weight_in.1, s32[3,12]{1,0:T(4,128)} %bitcast.7, ...), custom_call_target="tpu_custom_call" | custom-call | tf_op jit(solution)/shard_map/pallas_call | solution.py:574
  79.9 0.0 copy-start
  79.9 2.2 %copy.12 = bf16[4,4,16,1536]{3,2,1,0:T(8,128)(2,1)} copy(bf16[4,4,16,1536]{3,2,1,0:T(8,128)(2,1)} %bitcast.4) | data formatting | bytes 1572864
  82.1 0.0 copy-done
  82.1 0.0 copy-start.1
  82.1 1.1 %copy.13 = bf16[2,4,4,16,1536]{4,3,2,1,0:T(8,128)(2,1)} copy(bf16[2,4,4,16,1536]{4,3,2,1,0:T(8,128)(2,1)S(1)} %copy-done) | data formatting | bytes 3145728
  83.2 0.0 copy-done.1
  83.2 0.6 copy.14
Async XLA Ops:
  79.9 2.2 %copy-start = (bf16[2,4,4,16,1536]{4,3,2,1,0:T(8,128)(2,1)S(1)}, bf16[2,4,4,16,1536]{4,3,2,1,0:T(8,128)(2,1)}, u32[]{:S(2)}) copy-start(bf16[2,4,4,16,1536]{4,3,2,1,0:T(8,128)(2,1)} %get-tuple-element.13) | copy-start | bytes 4718596
  82.1 1.1 %copy-start.1 = (f32[6,2,1536]{2,1,0:T(2,128)S(1)}, f32[6,2,1536]{2,1,0:T(2,128)}, u32[]{:S(2)}) copy-start(f32[6,2,1536]{2,1,0:T(2,128)} %get-tuple-element.14) | copy-start | bytes 221188

commit v6 on v5

--- a/solution.py
+++ b/solution.py
@@ -507,8 +507,8 @@
     ring_a.middle()
     lax.fori_loop(3, 5, backward, 0)
     sides_1, inner_1 = frames_out(1)
+    inner_0.forward()
     rows_out(0, sides_0)
-    inner_0.forward()
     lax.fori_loop(5, 6, backward, 0)
     sides_2, inner_2 = frames_out(2)
     results = [pltpu.make_async_copy(dq, dq_out, local_sem.at[5])]
@@ -521,8 +521,9 @@
         for goal in range(2):
             second_a[half * 2 + goal] = block[:, goal * 384 : goal * 384 + 384].astype(bf16)
     sum_a.start()
+    inner_1.forward()
     rows_out(1, sides_1)
-    inner_1.forward()
+    inner_2.forward()
     pair_sums[1] = sum_b.end().astype(bf16)
     pair_sums[0] = sum_a.end().astype(bf16)
     low = start(pair_sums.at[1 - z_lo], pair_in, low_peer)
@@ -534,7 +535,6 @@
     for i in range(15):
         lasts.start(slots_out.at[(ha + i + 1) % 16], slots_in.at[ha], others[i])
     slots_in[ha] = slots_out[ha]
-    inner_2.forward()
     for i in range(2):
         dkv_out[i, :, 1:3] = dkv[i, 1:5, 2:4]
         for f, came in ((0, from_left), (3, from_right)):

time: 84 us -> 83.2 us (level)
  Pallas kernels: 79.3 us -> 78.2 us
    pallas_call x1, Pallas kernels: 79.3 us -> 78.2 us  [run_block(): pl.pallas_call(block_kernel, out_shape=[jax.ShapeDtypeStruct((256, 1536),...]
where the time goes in v6:
time: 83.2 us; the launch traced here: 82.9 us
  Pallas kernels  78.2 us (94%)
  local copies, waits for them, and re-layouts  3.96 us (5%)
    pallas_call x1, Pallas kernels, run_block(): pl.pallas_call(block_kernel, out_shape=[jax.ShapeDtypeStruct((256, 1536),...  78.2 us
    unnamed x7, local copies, waits for them, and re-layouts  3.96 us

profile of v6, /device:TPU:6, one launch (start us, length us, event | category | flops | bytes accessed | tf_op | source)
XLA Modules:
  0.0 82.9 jit_solution(13044252376093227713)
XLA Ops:
  0.6 78.2 %shard_map.85 = (bf16[256,1536]{1,0:T(8,128)(2,1)}, bf16[2,4,4,16,1536]{4,3,2,1,0:T(8,128)(2,1)}, f32[6,2,1536]{2,1,0:T(2,128)}) custom-call(bf16[256,1536]{1,0:T(8,128)(2,1)} %bitcast.5, bf16[2,4,4,16,1536]{4,3,2,1,0:T(8,128)(2,1)} %kv_in.1, bf16[256,1536]{1,0:T(8,128)(2,1)} %bitcast.6, bf16[96,1536]{1,0:T(8,128)(2,1)} %weight_in.1, s32[3,12]{1,0:T(4,128)} %bitcast.7, ...), custom_call_target="tpu_custom_call" | custom-call | tf_op jit(solution)/shard_map/pallas_call | solution.py:574
  78.9 0.0 copy-start
  78.9 2.2 %copy.12 = bf16[4,4,16,1536]{3,2,1,0:T(8,128)(2,1)} copy(bf16[4,4,16,1536]{3,2,1,0:T(8,128)(2,1)} %bitcast.4) | data formatting | bytes 1572864
  81.1 0.0 copy-done
  81.1 0.0 copy-start.1
  81.1 1.1 %copy.13 = bf16[2,4,4,16,1536]{4,3,2,1,0:T(8,128)(2,1)} copy(bf16[2,4,4,16,1536]{4,3,2,1,0:T(8,128)(2,1)S(1)} %copy-done) | data formatting | bytes 3145728
  82.2 0.0 copy-done.1
  82.2 0.6 copy.14
Async XLA Ops:
  78.9 2.2 %copy-start = (bf16[2,4,4,16,1536]{4,3,2,1,0:T(8,128)(2,1)S(1)}, bf16[2,4,4,16,1536]{4,3,2,1,0:T(8,128)(2,1)}, u32[]{:S(2)}) copy-start(bf16[2,4,4,16,1536]{4,3,2,1,0:T(8,128)(2,1)} %get-tuple-element.13) | copy-start | bytes 4718596
  81.1 1.1 %copy-start.1 = (f32[6,2,1536]{2,1,0:T(2,128)S(1)}, f32[6,2,1536]{2,1,0:T(2,128)}, u32[]{:S(2)}) copy-start(f32[6,2,1536]{2,1,0:T(2,128)} %get-tuple-element.14) | copy-start | bytes 221188

commit v7 on v6

--- a/solution.py
+++ b/solution.py
@@ -467,8 +467,9 @@
             first_a[goal, half] = block[goal * 96 : goal * 96 + 96]
     ring_a.start()
     gather_d.end()
+    gather_d.send(swaps, 2, 0, 4, partner)
     gather_y.end()
-    swap_parts(2)
+    gather_y.send(swaps, 2, 0, 4, partner)
     swaps.wait()
     weight_rows = weight.reshape(1536, 1536)
     inner, outer = pl.ds(2, 2), pl.ds(1, 2)

time: 83.2 us -> 83.3 us (level)
  no operation moved by 1% of the time
where the time goes in v7:
time: 83.3 us; the launch traced here: 82.9 us
  Pallas kernels  78.3 us (94%)
  local copies, waits for them, and re-layouts  3.96 us (5%)
    pallas_call x1, Pallas kernels, run_block(): pl.pallas_call(block_kernel, out_shape=[jax.ShapeDtypeStruct((256, 1536),...  78.3 us
    unnamed x7, local copies, waits for them, and re-layouts  3.96 us

profile of v7, /device:TPU:6, one launch (start us, length us, event | category | flops | bytes accessed | tf_op | source)
XLA Modules:
  0.0 82.9 jit_solution(16467478884621579106)
XLA Ops:
  0.6 78.3 %shard_map.85 = (bf16[256,1536]{1,0:T(8,128)(2,1)}, bf16[2,4,4,16,1536]{4,3,2,1,0:T(8,128)(2,1)}, f32[6,2,1536]{2,1,0:T(2,128)}) custom-call(bf16[256,1536]{1,0:T(8,128)(2,1)} %bitcast.5, bf16[2,4,4,16,1536]{4,3,2,1,0:T(8,128)(2,1)} %kv_in.1, bf16[256,1536]{1,0:T(8,128)(2,1)} %bitcast.6, bf16[96,1536]{1,0:T(8,128)(2,1)} %weight_in.1, s32[3,12]{1,0:T(4,128)} %bitcast.7, ...), custom_call_target="tpu_custom_call" | custom-call | tf_op jit(solution)/shard_map/pallas_call | solution.py:575
  78.9 0.0 copy-start
  79.0 2.2 %copy.12 = bf16[4,4,16,1536]{3,2,1,0:T(8,128)(2,1)} copy(bf16[4,4,16,1536]{3,2,1,0:T(8,128)(2,1)} %bitcast.4) | data formatting | bytes 1572864
  81.1 0.0 copy-done
  81.1 0.0 copy-start.1
  81.1 1.1 %copy.13 = bf16[2,4,4,16,1536]{4,3,2,1,0:T(8,128)(2,1)} copy(bf16[2,4,4,16,1536]{4,3,2,1,0:T(8,128)(2,1)S(1)} %copy-done) | data formatting | bytes 3145728
  82.3 0.0 copy-done.1
  82.3 0.6 copy.14
Async XLA Ops:
  78.9 2.2 %copy-start = (bf16[2,4,4,16,1536]{4,3,2,1,0:T(8,128)(2,1)S(1)}, bf16[2,4,4,16,1536]{4,3,2,1,0:T(8,128)(2,1)}, u32[]{:S(2)}) copy-start(bf16[2,4,4,16,1536]{4,3,2,1,0:T(8,128)(2,1)} %get-tuple-element.13) | copy-start | bytes 4718596
  81.1 1.1 %copy-start.1 = (f32[6,2,1536]{2,1,0:T(2,128)S(1)}, f32[6,2,1536]{2,1,0:T(2,128)}, u32[]{:S(2)}) copy-start(f32[6,2,1536]{2,1,0:T(2,128)} %get-tuple-element.14) | copy-start | bytes 221188
